TPU v7x, 32 devices: a whole 2x2x4 slice. The times are simulated.
32 devices in a mesh: groups: 2 (over x), tensor: 16 (over z, y, core).
Axes of the slice: x: 2, y: 2, z: 4, core: 2. Of those that a mesh axis runs over, the one named last changes fastest.
Arguments:
- tokens: bfloat16 [2048, 8192], P(('groups', 'tensor')), parts along dimension 0, may hold values from -6 to 6
- gate_weight: bfloat16 [8192, 28672], P(None, 'tensor'), may hold values from -0.0625 to 0.0625
- adapter_shrink: bfloat16 [32, 8192, 64], P(('groups', 'tensor')), parts along dimension 0, may hold values from -0.0625 to 0.0625
- adapter_expand: bfloat16 [32, 64, 28672], P(('groups', 'tensor')), parts along dimension 0, may hold values from -0.75 to 0.75
- adapter_blocks: int32 [32], P('groups'), parts along dimension 0, may hold values from 1 to 4, 32 in all
- adapter_position: int32 [32], P('groups'), parts along dimension 0, may hold values from 0 to 15, each once
Outputs:
- projected: bfloat16 [2048, 28672], P('groups', 'tensor'), parts along dimension 0
There are 2 independent parts, one for each index of `groups`. A program takes and returns all parts, laid end to end along the dimension named above; an argument that names none is the same for every part. Nothing has to cross between parts.
Inputs may be any that keep to these rules, and one draw needn't show every extreme that they name: Adapter k serves the 32-row blocks that follow those of adapters 0 to k-1, adapter_blocks[k] of them; some adapter serves exactly 4. Each storage position holds exactly one adapter; adapter k is stored on the device of index adapter_position[k] along tensor.
All inputs are finite; a program needn't handle non-finite values.
Results may differ from a plain program's by a relative error of at most 0.005.
Values may be sent and summed in bfloat16 or wider, within the bound.
No kernel may reach another device: no remote copies, remote signals or barrier semaphores. Data moves between devices by JAX's collectives and lax.ppermute only.
A program may use at most 192 MiB of HBM per device.

v0:
```python
import jax
import jax.numpy as jnp
from jax import lax
from jax.sharding import PartitionSpec as P

BLOCK = 32


def local(tokens, gate_weight, adapter_shrink, adapter_expand, adapter_blocks, adapter_position):
    width = lax.axis_size("tensor")
    my_index = lax.axis_index("tensor")
    local_rows = tokens.shape[0]
    gathered_rows = local_rows * width
    column_width = gate_weight.shape[1]
    adapter_count = adapter_position.shape[0]
    num_blocks = gathered_rows // BLOCK
    seg_ends = jnp.cumsum(adapter_blocks)
    seg_starts = (seg_ends - adapter_blocks) * BLOCK
    blocks = jnp.arange(num_blocks, dtype=jnp.int32)
    block_adapter = jnp.sum((blocks[:, None] >= seg_ends[None, :]).astype(jnp.int32), axis=1)
    adapter_ids = jnp.arange(adapter_count, dtype=jnp.int32)
    block_onehot = (block_adapter[:, None] == adapter_ids[None, :]).astype(jnp.int32)
    block_position = jnp.sum(block_onehot * adapter_position[None, :], axis=1)
    row_mine = jnp.repeat(block_position == my_index, BLOCK)
    shrunk_local = adapter_shrink[0]
    piece = lax.all_gather(tokens, "tensor", axis=0, tiled=True)
    base_part = jnp.dot(piece, gate_weight, preferred_element_type=jnp.float32)
    shrink_part = jnp.dot(piece, shrunk_local, preferred_element_type=jnp.float32)
    shrink_part = jnp.where(row_mine[:, None], shrink_part, 0.0)
    combined = jnp.concatenate([base_part, shrink_part], axis=1)
    base_output = combined[:, :column_width]
    shrink_mine = combined[:, column_width:]
    capacity = 2 * local_rows
    begins = jnp.minimum(seg_starts, gathered_rows - capacity)
    slot_onehot = (adapter_position[:, None] == adapter_ids[None, :]).astype(jnp.int32)
    begin_by_slot = jnp.sum(slot_onehot * begins[:, None], axis=0)
    my_begin = jnp.sum(jnp.where(adapter_ids == my_index, begin_by_slot, 0))
    chosen_rows = lax.dynamic_slice_in_dim(shrink_mine, my_begin, capacity, 0).astype(jnp.bfloat16)
    expanded_rows = jnp.dot(
        chosen_rows, adapter_expand[0], preferred_element_type=jnp.float32
    ).astype(jnp.bfloat16)
    received = lax.all_to_all(
        expanded_rows.reshape(capacity, width, column_width),
        "tensor",
        split_axis=1,
        concat_axis=0,
        tiled=True,
    )
    flattened_rows = received.reshape(width * capacity, column_width)
    destination_rows = (
        begin_by_slot[:, None] + jnp.arange(capacity, dtype=jnp.int32)[None, :]
    ).reshape(-1)
    adapter_output = (
        jnp.zeros((gathered_rows, column_width), jnp.bfloat16)
        .at[destination_rows]
        .add(flattened_rows)
    )
    adapter_output = lax.optimization_barrier(adapter_output)
    return (base_output + adapter_output.astype(jnp.float32)).astype(jnp.bfloat16)


def solution(mesh):
    return jax.shard_map(
        local,
        mesh=mesh,
        in_specs=(
            P(("groups", "tensor"), None),
            P(None, "tensor"),
            P(("groups", "tensor"), None, None),
            P(("groups", "tensor"), None, None),
            P("groups"),
            P("groups"),
        ),
        out_specs=P("groups", "tensor"),
        check_vma=False,
    )
```

profile of v0, /device:TPU:13, one launch (start us, length us, event | category | flops | bytes accessed | tf_op | source)
XLA Modules:
  0.0 394.2 jit_solution(9006662242983685787)
XLA Ops:
  6.5 0.0 copy-start
  6.5 0.0 all-gather.2.cloned.1.call-start
  6.5 0.7 all-gather.2.cloned.1.call-update
  7.3 0.7 copy.11
  8.0 0.1 reduce
  8.2 0.7 multiply_minimum_fusion
  8.8 0.7 select_reduce_fusion.1
  9.6 0.6 fusion.9
  11.5 0.1 convert_reduce_fusion
  11.6 0.7 select_reduce_fusion
  12.3 0.1 broadcast_in_dim.36
  12.4 0.1 broadcast_in_dim.37
  13.2 0.1 dynamic-slice
  13.2 121.9 %all-gather.2.cloned.1.call-done = bf16[1024,8192]{1,0:T(8,128)(2,1)} async-done(((bf16[64,8192]{1,0:T(8,128)(2,1)}), bf16[1024,8192]{1,0:T(8,128)(2,1)}) %all-gather.2.cloned.1.call-update) | async-done | bytes 16777232 | tf_op jit(solution)/shard_map/all_gather | solution.py:26
  135.1 0.0 copy-done
  135.1 0.0 copy-start.2
  135.1 11.1 %fusion.3 = bf16[1024,64]{0,1:T(8,128)(2,1)S(1)} fusion(bf16[1024,8192]{1,0:T(8,128)(2,1)} %all-gather.2.cloned.1.call-done, bf16[1,8192,64]{1,2,0:T(8,128)(2,1)S(1)} %copy-done), kind=kOutput, calls=%fused_computation.7 | convolution fusion | flops 1073741824 | bytes 17956864 | tf_op jit(solution)/shard_map/dot_general | solution.py:28
  146.2 0.0 copy-done.2
  146.2 2.2 convolution_convert_fusion
  148.4 3.8 copy.15
  152.2 7.7 %all-to-all-start = ((bf16[128,16,1792]{2,0,1:T(8,128)(2,1)}), bf16[128,16,1792]{2,0,1:T(8,128)(2,1)}, u32[]{:S(2)}, u32[]{:S(2)}) async-start(bf16[128,16,1792]{2,0,1:T(8,128)(2,1)} %bitcast.21), calls=%async_computation | async-start | bytes 14680064 | tf_op jit(solution)/shard_map/all_to_all | solution.py:42
  160.0 0.1 iota_add_fusion
  160.0 159.8 %all-to-all-done = bf16[128,16,1792]{2,0,1:T(8,128)(2,1)} async-done(((bf16[128,16,1792]{2,0,1:T(8,128)(2,1)}), bf16[128,16,1792]{2,0,1:T(8,128)(2,1)}, u32[]{:S(2)}, u32[]{:S(2)}) %all-to-all-start) | async-done | bytes 7340064 | tf_op jit(solution)/shard_map/all_to_all | solution.py:42
  319.9 27.8 %scatter_custom_fusion = bf16[1024,1792]{1,0:T(8,128)(2,1)} fusion(s32[2048]{0:T(1024)S(1)} %bitcast.24, bf16[2048,1792]{1,0:T(8,128)(2,1)} %bitcast.7, bf16[]{:T(256)} %constant.7.clone.1), kind=kCustom, calls=%fused_computation.5 | custom fusion | flops 3670016 | bytes 3670528 | tf_op jit(solution)/shard_map/scatter-add | solution.py:56
  347.7 0.0 copy-start.1
  347.7 39.6 %add_convert_fusion = bf16[1024,1792]{1,0:T(8,128)(2,1)} fusion(bf16[1024,1792]{1,0:T(8,128)(2,1)} %scatter_custom_fusion, bf16[1024,8192]{1,0:T(8,128)(2,1)} %all-gather.2.cloned.1.call-done, bf16[8192,1792]{1,0:T(8,128)(2,1)} %param.7), kind=kOutput, calls=%fused_computation.3 | convolution fusion | flops 30070276096 | bytes 53477376 | tf_op jit(solution)/shard_map/dot_general | solution.py:27
  387.3 0.0 copy-done.1
  (3 shorter events, 0.1 us)
Async XLA Ops:
  6.5 128.6 %copy-start = (bf16[1,8192,64]{1,2,0:T(8,128)(2,1)S(1)}, bf16[1,8192,64]{1,2,0:T(8,128)(2,1)}, u32[]{:S(2)}) copy-start(bf16[1,8192,64]{1,2,0:T(8,128)(2,1)} %param.8) | copy-start | bytes 3145732
  6.5 128.6 %all-gather.2.cloned.1.call-start = ((), (), s32[]{:S(2)}) async-start(), calls=%async_computation.1 | async-start | bytes 17825792 | tf_op jit(solution)/shard_map/all_gather | solution.py:26
  135.1 11.1 %copy-start.2 = (bf16[1,64,28672]{2,1,0:T(8,128)(2,1)S(1)}, bf16[1,64,28672]{2,1,0:T(8,128)(2,1)}, u32[]{:S(2)}) copy-start(bf16[1,64,28672]{2,1,0:T(8,128)(2,1)} %param.9) | copy-start | bytes 11010052
  152.2 167.6 %all-to-all-start = ((bf16[128,16,1792]{2,0,1:T(8,128)(2,1)}), bf16[128,16,1792]{2,0,1:T(8,128)(2,1)}, u32[]{:S(2)}, u32[]{:S(2)}) async-start(bf16[128,16,1792]{2,0,1:T(8,128)(2,1)} %bitcast.21), calls=%async_computation | async-start | bytes 14680064 | tf_op jit(solution)/shard_map/all_to_all | solution.py:42
  347.7 39.6 %copy-start.1 = (bf16[1,8192,64]{1,2,0:T(8,128)(2,1)S(1)}, bf16[1,8192,64]{1,2,0:T(8,128)(2,1)}, u32[]{:S(2)}) copy-start(bf16[1,8192,64]{1,2,0:T(8,128)(2,1)} %param.8) | copy-start | bytes 3145732
Sparse Core Ops, SparseCore 0:
  9.5 125.5 all-gather.1
where the time goes:
time: 394 us
  waiting for transfers between devices  282 us (72%)
  matrix products  52.9 us (13%)
  other arithmetic  30.9 us (8%)
  between operations  15.4 us (4%)
  starting transfers between devices  7.74 us (2%)
  local copies, waits for them, and re-layouts  4.77 us (1%)
    all_to_all x1, waiting for transfers between devices, local(): lax.all_to_all(expanded_rows.reshape(capacity, width, column_width), 'ten...  160 us
    all_gather x1, waiting for transfers between devices, local(): piece = lax.all_gather(tokens, 'tensor', axis=0, tiled=True)  122 us
    dot_general x1, matrix products, local(): base_part = jnp.dot(piece, gate_weight, preferred_element_type=jnp.float32)  39.6 us
    scatter-add x1, other arithmetic, local(): adapter_output = jnp.zeros((gathered_rows, column_width), jnp.bfloat16).a...  27.8 us
    dot_general x1, matrix products, local(): jnp.dot(piece, shrunk_local, preferred_element_type=jnp.float32)  11.1 us
  transfers between devices with their start and end apart: 2, of which 2 were waited for; matrix products, arithmetic and copies ran while one was open for 1% of the time, Pallas kernels for 0%

commit v1 on v0

v1 whole, which is shorter than its diff:
```python
import functools

import jax
import jax.numpy as jnp
from jax import lax
from jax.experimental import pallas as pl
from jax.experimental.pallas import tpu as pltpu
from jax.sharding import PartitionSpec as P

BLOCK = 32
MOST = 4
AXIS = "tensor"
VMEM_LIMIT = 56 * 1024 * 1024
ANY = pl.BlockSpec(memory_space=pl.ANY)


def tie(values, after):
    count = len(values)

    def body(*refs):
        del refs

    return pl.pallas_call(
        body,
        out_shape=[jax.ShapeDtypeStruct(v.shape, v.dtype) for v in values],
        in_specs=[ANY] * (count + len(after)),
        out_specs=[ANY] * count,
        input_output_aliases={i: i for i in range(count)},
        name="tie",
    )(*values, *after)


def plane_kernel(pieces, fill, scalars, *refs):
    sources = refs[:pieces]
    weight, shrink_t = refs[pieces : pieces + 2]
    out, shrunk, rows, sem = refs[-4:]

    @pl.when(pl.program_id(0) == 0)
    def _():
        fill(scalars, sources, rows, sem)
        s = lax.dot_general(
            rows[...], shrink_t[...], (((1,), (1,)), ((), ())), preferred_element_type=jnp.float32
        ).astype(shrunk.dtype)
        shrunk[...] = jnp.concatenate([s, jnp.zeros_like(s)], axis=1)

    out[...] = jnp.dot(rows[...], weight[...], preferred_element_type=jnp.float32)


def plane_matmul(fill, scalars, sources, weight, shrink_t, held, total_rows, plane_rows, tile=256):
    depth, columns = weight.shape
    rank = shrink_t.shape[0]
    pieces = len(sources)
    aliases = {} if held is None else {1 + pieces + 2: 0, 1 + pieces + 3: 1}
    extra = () if held is None else tuple(held)
    while columns % tile:
        tile //= 2
    return pl.pallas_call(
        functools.partial(plane_kernel, pieces, fill),
        out_shape=[
            jax.ShapeDtypeStruct((total_rows, columns), jnp.float32),
            jax.ShapeDtypeStruct((total_rows, 2 * rank), jnp.bfloat16),
        ],
        grid_spec=pltpu.PrefetchScalarGridSpec(
            num_scalar_prefetch=1,
            grid=(columns // tile,),
            in_specs=[ANY] * pieces
            + [
                pl.BlockSpec((depth, tile), lambda n, s: (0, n)),
                pl.BlockSpec((rank, depth), lambda n, s: (0, 0)),
            ]
            + [ANY] * len(extra),
            out_specs=[
                pl.BlockSpec((plane_rows, tile), lambda n, s: (s[0], n)),
                pl.BlockSpec((plane_rows, 2 * rank), lambda n, s: (s[0], 0)),
            ],
            scratch_shapes=[pltpu.VMEM((plane_rows, depth), jnp.bfloat16), pltpu.SemaphoreType.DMA((2,))],
        ),
        input_output_aliases=aliases,
        compiler_params=pltpu.CompilerParams(vmem_limit_bytes=VMEM_LIMIT),
        cost_estimate=pl.CostEstimate(
            flops=2 * plane_rows * depth * columns,
            bytes_accessed=2 * depth * columns + 2 * plane_rows * depth + 4 * plane_rows * columns,
            transcendentals=0,
        ),
        name="plane",
    )(scalars, *sources, weight, shrink_t, *extra)


def fill_own(shard, scalars, sources, rows, sem):
    chip, across, across_other = sources
    y, core = scalars[1], scalars[2]
    other = (1 - y) * 2 * shard
    first = pltpu.make_async_copy(chip, rows.at[pl.ds(pl.multiple_of(y * 2 * shard, 2 * shard), 2 * shard)], sem.at[0])
    first.start()
    first.wait()
    second = pltpu.make_async_copy(
        across, rows.at[pl.ds(pl.multiple_of(other + core * shard, shard), shard)], sem.at[0]
    )
    third = pltpu.make_async_copy(
        across_other, rows.at[pl.ds(pl.multiple_of(other + (1 - core) * shard, shard), shard)], sem.at[1]
    )
    second.start()
    third.start()
    second.wait()
    third.wait()


def fill_far(shard, scalars, sources, rows, sem):
    y, chosen = scalars[1], scalars[3]
    mine = pl.ds(pl.multiple_of(y * 2 * shard, 2 * shard), 2 * shard)
    others = pl.ds(pl.multiple_of((1 - y) * 2 * shard, 2 * shard), 2 * shard)
    for i in range(len(sources) // 2):

        @pl.when(chosen == i)
        def _():
            first = pltpu.make_async_copy(sources[2 * i], rows.at[mine], sem.at[0])
            second = pltpu.make_async_copy(sources[2 * i + 1], rows.at[others], sem.at[1])
            first.start()
            second.start()
            first.wait()
            second.wait()


def last_kernel(slots, rank, begins, base, shrunk, expand, out, spread):
    capacity = shrunk.shape[1]

    @pl.when(pl.program_id(0) == 0)
    def _():
        spread[...] = jnp.zeros_like(spread)
        for s in range(slots):
            rows = pl.ds(pl.multiple_of(begins[s], BLOCK), capacity)
            spread[rows, s * rank : (s + 1) * rank] = shrunk[s, :, :rank]

    lora = jnp.dot(spread[...], expand[...], preferred_element_type=jnp.float32).astype(jnp.bfloat16)
    out[...] = (base[...] + lora.astype(jnp.float32)).astype(jnp.bfloat16)


def last(begins, base, shrunk, expand, rank, tile=256):
    total_rows, columns = base.shape
    slots, capacity, wide = shrunk.shape
    while columns % tile:
        tile //= 2
    return pl.pallas_call(
        functools.partial(last_kernel, slots, rank),
        out_shape=jax.ShapeDtypeStruct((total_rows, columns), jnp.bfloat16),
        grid_spec=pltpu.PrefetchScalarGridSpec(
            num_scalar_prefetch=1,
            grid=(columns // tile,),
            in_specs=[
                pl.BlockSpec((total_rows, tile), lambda n, s: (0, n)),
                pl.BlockSpec((slots, capacity, wide), lambda n, s: (0, 0, 0)),
                pl.BlockSpec((slots * rank, tile), lambda n, s: (0, n)),
            ],
            out_specs=pl.BlockSpec((total_rows, tile), lambda n, s: (0, n)),
            scratch_shapes=[pltpu.VMEM((total_rows, slots * rank), jnp.bfloat16)],
        ),
        compiler_params=pltpu.CompilerParams(vmem_limit_bytes=VMEM_LIMIT),
        cost_estimate=pl.CostEstimate(
            flops=2 * total_rows * slots * rank * columns,
            bytes_accessed=6 * total_rows * columns + 2 * slots * rank * columns,
            transcendentals=0,
        ),
        name="last",
    )(begins, base, shrunk, expand)


def local(tokens, gate_weight, adapter_shrink, adapter_expand, adapter_blocks, adapter_position):
    width = lax.axis_size(AXIS)
    me = lax.axis_index(AXIS)
    shard, depth = tokens.shape
    columns = gate_weight.shape[1]
    rank = adapter_shrink.shape[2]
    total_rows = shard * width
    plane_rows = 4 * shard
    planes = width // 4
    z, y, core = me // 4, (me // 2) % 2, me % 2

    count = adapter_position.shape[0]
    ids = jnp.arange(count, dtype=jnp.int32)
    capacity = MOST * BLOCK
    starts = jnp.sum(jnp.where(ids[None, :] < ids[:, None], adapter_blocks[None, :], 0), axis=1) * BLOCK
    sizes = adapter_blocks * BLOCK
    at_slot = adapter_position[None, :] == ids[:, None]
    start_by_slot = jnp.sum(jnp.where(at_slot, starts[None, :], 0), axis=1)
    size_by_slot = jnp.sum(jnp.where(at_slot, sizes[None, :], 0), axis=1)
    begin_by_slot = jnp.minimum(start_by_slot, total_rows - capacity)

    def at(z_, y_, c_):
        return (z_ * 2 + y_) * 2 + c_

    both = [(a, b, c) for a in range(planes) for b in range(2) for c in range(2)]
    swap_core = [(at(a, b, c), at(a, b, 1 - c)) for a, b, c in both]
    swap_y = [(at(a, b, c), at(a, 1 - b, c)) for a, b, c in both]

    def holds(j, a, c):
        return a >= j if c == 0 else a <= planes - 1 - j

    def along(j):
        up = [(at(a, b, 0), at(a + 1, b, 0)) for a in range(j - 1, planes - 1) for b in range(2)]
        down = [(at(a, b, 1), at(a - 1, b, 1)) for a in range(1, planes - j + 1) for b in range(2)]
        return up + down

    def send(value, pairs):
        return lax.ppermute(value, AXIS, pairs)

    expand_parts = adapter_expand.reshape(rank, width, columns).transpose(1, 0, 2)
    expand = lax.all_to_all(expand_parts, AXIS, split_axis=0, concat_axis=0, tiled=True)

    other_core = send(tokens, swap_core)
    across = send(tokens, swap_y)
    chip = jnp.where(
        core == 0, jnp.concatenate([tokens, other_core]), jnp.concatenate([other_core, tokens])
    )
    across_other = send(across, swap_core)

    shrink_t = jnp.swapaxes(adapter_shrink[0], 0, 1)
    scalars = jnp.stack([z, y, core, 0]).astype(jnp.int32)
    held = plane_matmul(
        functools.partial(fill_own, shard), scalars, [chip, across, across_other], gate_weight, shrink_t, None,
        total_rows, plane_rows,
    )

    order = []
    for a in range(planes):
        found = []
        for j in range(1, planes):
            if a >= j:
                found.append((a - j, j, 0))
            if a <= planes - 1 - j:
                found.append((a + j, j, 1))
        order.append(found)
    table = jnp.asarray(
        [[[p, 2 * (j - 1) + d] for p, j, d in found] for found in order], jnp.int32
    )
    mine = lax.dynamic_index_in_dim(table, z, 0, keepdims=False)

    sources = []
    carried = chip
    for j in range(1, planes):
        swap_yj = [(at(a, b, c), at(a, 1 - b, c)) for a, b, c in both if holds(j, a, c)]
        swap_cj = [(at(a, b, c), at(a, b, 1 - c)) for a, b, c in both if holds(j, a, c)]
        carried = send(carried, along(j))
        carried_across = send(carried, swap_yj)
        sources += [carried, carried_across, send(carried, swap_cj), send(carried_across, swap_cj)]
        pick = mine[j - 1, 1]
        pick = pick - pick % 2 + jnp.where(pick % 2 == core, 0, 1)
        scalars = jnp.stack([mine[j - 1, 0], y, core, pick]).astype(jnp.int32)
        held = plane_matmul(
            functools.partial(fill_far, shard), scalars, list(sources), gate_weight, shrink_t, held,
            total_rows, plane_rows,
        )
    base, shrunk = held

    my_begin, my_start, my_size = begin_by_slot[me], start_by_slot[me], size_by_slot[me]
    rows = my_begin + jnp.arange(capacity, dtype=jnp.int32)
    keep = (rows >= my_start) & (rows < my_start + my_size)
    chosen = lax.dynamic_slice_in_dim(shrunk, my_begin, capacity, 0)
    chosen = jnp.where(keep[:, None], chosen, jnp.zeros_like(chosen))
    chosen = jnp.broadcast_to(chosen[None], (width, capacity, 2 * rank))
    shrunk_all = lax.all_to_all(chosen, AXIS, split_axis=0, concat_axis=0, tiled=True)
    return last(begin_by_slot, base, shrunk_all, expand.reshape(width * rank, columns), rank)


def solution(mesh):
    return jax.shard_map(
        local,
        mesh=mesh,
        in_specs=(
            P(("groups", "tensor"), None),
            P(None, "tensor"),
            P(("groups", "tensor"), None, None),
            P(("groups", "tensor"), None, None),
            P("groups"),
            P("groups"),
        ),
        out_specs=P("groups", "tensor"),
        check_vma=False,
    )
```

time: 394 us -> 337 us (0.86)
  waiting for transfers between devices: 282 us -> 155 us
  Pallas kernels: 0 us -> 92 us
  matrix products: 52.9 us -> 0 us
  starting transfers between devices: 7.74 us -> 38.5 us
  other arithmetic: 30.9 us -> 8.59 us
  blocking collectives: 0 us -> 18.9 us
  local copies, waits for them, and re-layouts: 4.77 us -> 8.89 us
  between operations: 15.4 us -> 11.3 us
    all_to_all x1, waiting for transfers between devices: 160 us -> 0.01 us  [local(): lax.all_to_all(expand_parts, AXIS, split_axis=0, concat_axis=0, tiled=True)]
    ppermute x0 -> x15, waiting for transfers between devices: none -> 155 us  [send(): return lax.ppermute(value, AXIS, pairs)]
    all_gather x1 -> x0, waiting for transfers between devices: 122 us -> none  [local(): piece = lax.all_gather(tokens, 'tensor', axis=0, tiled=True)]
    pallas_call x0 -> x5, Pallas kernels: none -> 92 us  [the longest x4 81.1 us: plane_matmul(): pl.pallas_call(functools.partial(plane_kernel, pieces, fill), out_shape=[...]
    dot_general x3 -> x0, matrix products: 52.9 us -> none  [the longest x1 39.6 us: local(): base_part = jnp.dot(piece, gate_weight, preferred_element_type=jnp.float32)]
    ppermute x0 -> x15, starting transfers between devices: none -> 29.6 us  [send(): return lax.ppermute(value, AXIS, pairs)]
    scatter-add x1 -> x0, other arithmetic: 27.8 us -> none  [local(): adapter_output = jnp.zeros((gathered_rows, column_width), jnp.bfloat16).a...]
    all_to_all x0 -> x1, blocking collectives: none -> 18.9 us  [local(): lax.all_to_all(chosen, AXIS, split_axis=0, concat_axis=0, tiled=True)]
  transfers between devices with their start and end apart: 2 -> 16, of which waited for: 2 -> 6; matrix products, arithmetic and copies ran while one was open for 1% -> 4% of each run, Pallas kernels for 0% -> 24%
where the time goes in v1:
time: 337 us; the launch traced here: 333 us
  waiting for transfers between devices  155 us (46%)
  Pallas kernels  92 us (27%)
  starting transfers between devices  38.5 us (11%)
  blocking collectives  18.9 us (6%)
  between operations  11.3 us (3%)
  local copies, waits for them, and re-layouts  8.89 us (3%)
  other arithmetic  8.59 us (3%)
    ppermute x15, waiting for transfers between devices, send(): return lax.ppermute(value, AXIS, pairs)  155 us
    pallas_call x4, Pallas kernels, plane_matmul(): pl.pallas_call(functools.partial(plane_kernel, pieces, fill), out_shape=[...  81.1 us
    ppermute x15, starting transfers between devices, send(): return lax.ppermute(value, AXIS, pairs)  29.6 us
    all_to_all x1, blocking collectives, local(): lax.all_to_all(chosen, AXIS, split_axis=0, concat_axis=0, tiled=True)  18.9 us
    pallas_call x1, Pallas kernels, last(): pl.pallas_call(functools.partial(last_kernel, slots, rank), out_shape=jax...  11 us
    all_to_all x1, starting transfers between devices, local(): lax.all_to_all(expand_parts, AXIS, split_axis=0, concat_axis=0, tiled=True)  8.94 us
  transfers between devices with their start and end apart: 16, of which 6 were waited for; matrix products, arithmetic and copies ran while one was open for 4% of the time, Pallas kernels for 24%

profile of v1, /device:TPU:13, one launch (start us, length us, event | category | flops | bytes accessed | tf_op | source)
XLA Modules:
  0.0 333.3 jit_solution(14302059203249097329)
XLA Ops:
  0.7 2.5 collective-permute-done
  3.2 2.0 maximum_select_fusion.refs_0_
  5.2 2.1 collective-permute-start.1
  7.3 25.0 %collective-permute-done.1.refs_0_ = bf16[128,8192]{1,0:T(8,128)(2,1)S(1)} collective-permute-done((bf16[128,8192]{1,0:T(8,128)(2,1)S(1)}, bf16[128,8192]{1,0:T(8,128)(2,1)S(1)}, u32[]{:S(2)}, u32[]{:S(2)}) %collective-permute-start.1) | collective-permute-done | bytes 2097184 | tf_op jit(solution)/shard_map/ppermute | solution.py:204
  32.3 1.9 collective-permute-start.5
  34.2 25.0 %collective-permute-done.5.refs_4_ = bf16[128,8192]{1,0:T(8,128)(2,1)} collective-permute-done((bf16[128,8192]{1,0:T(8,128)(2,1)S(1)}, bf16[128,8192]{1,0:T(8,128)(2,1)}, u32[]{:S(2)}, u32[]{:S(2)}) %collective-permute-start.5) | collective-permute-done | bytes 2097184 | tf_op jit(solution)/shard_map/ppermute | solution.py:204
  59.2 3.2 collective-permute-start.9
  63.1 2.9 copy.18
  66.1 8.9 %all-to-all-start.1 = ((bf16[16,64,1792]{2,1,0:T(8,128)(2,1)}), bf16[16,64,1792]{2,1,0:T(8,128)(2,1)}, u32[]{:S(2)}, u32[]{:S(2)}) async-start(bf16[16,64,1792]{2,1,0:T(8,128)(2,1)} %bitcast.31), calls=%async_computation.1 | async-start | bytes 7340032 | tf_op jit(solution)/shard_map/all_to_all | solution.py:207
  75.0 2.2 collective-permute-start.2
  77.2 1.2 collective-permute-start.13
  78.5 2.2 collective-permute-start.6
  80.7 2.6 collective-permute-start.3
  83.3 33.6 %collective-permute-done.9.refs_8_ = bf16[128,8192]{1,0:T(8,128)(2,1)} collective-permute-done((bf16[128,8192]{1,0:T(8,128)(2,1)}, bf16[128,8192]{1,0:T(8,128)(2,1)}, u32[]{:S(2)}, u32[]{:S(2)}) %collective-permute-start.9) | collective-permute-done | bytes 2097184 | tf_op jit(solution)/shard_map/ppermute | solution.py:204
  116.9 2.0 collective-permute-start.10
  118.9 64.2 %collective-permute-done.13.refs_1_ = bf16[64,8192]{1,0:T(8,128)(2,1)} collective-permute-done((bf16[64,8192]{1,0:T(8,128)(2,1)S(1)}, bf16[64,8192]{1,0:T(8,128)(2,1)}, u32[]{:S(2)}, u32[]{:S(2)}) %collective-permute-start.13) | collective-permute-done | bytes 1048608 | tf_op jit(solution)/shard_map/ppermute | solution.py:204
  183.1 1.3 collective-permute-start.14
  184.5 1.9 collective-permute-start.4
  197.1 3.8 %collective-permute-start.7 = (bf16[128,8192]{1,0:T(8,128)(2,1)}, bf16[128,8192]{1,0:T(8,128)(2,1)}, u32[]{:S(2)}, u32[]{:S(2)}) collective-permute-start(bf16[128,8192]{1,0:T(8,128)(2,1)} %collective-permute-done.5.refs_4_), channel_id=1, source_target_pairs={{1,0},{3,2},{5,4},{7,6},{8,9},{10,11},{12,13},{14,15},{17,16},{19,... | collective-permute-start | bytes 6291464 | tf_op jit(solution)/shard_map/ppermute | solution.py:204
  200.9 4.8 %collective-permute-done.6.refs_5_ = bf16[128,8192]{1,0:T(8,128)(2,1)} collective-permute-done((bf16[128,8192]{1,0:T(8,128)(2,1)}, bf16[128,8192]{1,0:T(8,128)(2,1)}, u32[]{:S(2)}, u32[]{:S(2)}) %collective-permute-start.6) | collective-permute-done | bytes 2097184 | tf_op jit(solution)/shard_map/ppermute | solution.py:204
  205.8 2.6 collective-permute-start.8
  212.0 1.2 compare_and_fusion
  213.8 1.2 pad_add_fusion.2.scalars
  215.0 1.2 pad_add_fusion.1.scalars
  216.3 1.2 pad_add_fusion.scalars
  219.3 21.0 %plane.4 = (f32[1024,1792]{1,0:T(8,128)}, bf16[1024,128]{1,0:T(8,128)(2,1)}) custom-call(s32[4]{0:T(128)} %pad_add_fusion.3.scalars, bf16[128,8192]{1,0:T(8,128)(2,1)} %copy-done.1, bf16[64,8192]{1,0:T(8,128)(2,1)} %collective-permute-done.13.refs_1_, bf16[64,8192]{1,0:T(8,128)(2,1)} %copy-done.6, bf16[8192,1792]{1,0:T(8,128)(2,1)} %refs_12_.1, ...), custom_call_target="tpu_custom_call" | custom-call | flops 7516192768 | bytes 35389440 | tf_op jit(solution)/shard_map/plane/pallas_call | solution.py:57
  240.3 20.0 %plane.5 = (f32[1024,1792]{1,0:T(8,128)}, bf16[1024,128]{1,0:T(8,128)(2,1)}) custom-call(s32[4]{0:T(128)} %pad_add_fusion.2.scalars, bf16[128,8192]{1,0:T(8,128)(2,1)} %copy-done, bf16[128,8192]{1,0:T(8,128)(2,1)} %collective-permute-done.2.refs_1_, bf16[128,8192]{1,0:T(8,128)(2,1)} %collective-permute-done.3.refs_2_, ...), custom_call_target="tpu_custom_call", output_to_operand_aliasing={{0}: (7, {}), {1}: (8, {})} | custom-call | flops 7516192768 | bytes 35389440 | tf_op jit(solution)/shard_map/plane/pallas_call | solution.py:57
  260.3 20.0 %plane.6 = (f32[1024,1792]{1,0:T(8,128)}, bf16[1024,128]{1,0:T(8,128)(2,1)}) custom-call(s32[4]{0:T(128)} %pad_add_fusion.1.scalars, bf16[128,8192]{1,0:T(8,128)(2,1)} %copy-done, bf16[128,8192]{1,0:T(8,128)(2,1)} %collective-permute-done.2.refs_1_, ...), custom_call_target="tpu_custom_call", output_to_operand_aliasing={{0}: (11, {}), {1}: (12, {})} | custom-call | flops 7516192768 | bytes 35389440 | tf_op jit(solution)/shard_map/plane/pallas_call | solution.py:57
  280.4 1.3 copy-done.3
  282.4 20.0 %plane.7 = (f32[1024,1792]{1,0:T(8,128)}, bf16[1024,128]{1,0:T(8,128)(2,1)}) custom-call(s32[4]{0:T(128)} %pad_add_fusion.scalars, bf16[128,8192]{1,0:T(8,128)(2,1)} %copy-done, bf16[128,8192]{1,0:T(8,128)(2,1)} %collective-permute-done.2.refs_1_, bf16[128,8192]{1,0:T(8,128)(2,1)} %collective-permute-done.3.refs_2_, ...), custom_call_target="tpu_custom_call", output_to_operand_aliasing={{0}: (15, {}), {1}: (16, {})} | custom-call | flops 7516192768 | bytes 35389440 | tf_op jit(solution)/shard_map/plane/pallas_call | solution.py:57
  303.4 18.9 %all_to_all.10.shrunk = bf16[16,128,128]{2,1,0:T(8,128)(2,1)} all-to-all(bf16[16,128,128]{2,1,0:T(8,128)(2,1)S(1)} %broadcast_in_dim.55), channel_id=1, replica_groups=mesh['groups'=2,'tensor'=16] {'tensor'}, dimensions={0} | all-to-all | bytes 1048576 | tf_op jit(solution)/shard_map/all_to_all | solution.py:260
  322.3 11.0 %last.1 = bf16[1024,1792]{1,0:T(8,128)(2,1)} custom-call(s32[16]{0:T(128)} %copy-done.7, f32[1024,1792]{1,0:T(8,128)} %get-tuple-element.19.base, bf16[16,128,128]{2,1,0:T(8,128)(2,1)} %all_to_all.10.shrunk, bf16[1024,1792]{1,0:T(8,128)(2,1)} %bitcast.20.expand), custom_call_target="tpu_custom_call" | custom-call | flops 3758096384 | bytes 14680064 | tf_op jit(solution)/shard_map/last/pallas_call | solution.py:143
  (45 shorter events, 8.8 us)
Async XLA Ops:
  0.0 3.2 collective-permute-start
  0.7 61.7 %copy-start.2 = (bf16[1,64,28672]{2,1,0:T(8,128)(2,1)S(1)}, bf16[1,64,28672]{2,1,0:T(8,128)(2,1)}, u32[]{:S(2)}) copy-start(bf16[1,64,28672]{2,1,0:T(8,128)(2,1)} %param.10) | copy-start | bytes 11010052
  5.2 57.2 %copy-start.1 = (bf16[128,8192]{1,0:T(8,128)(2,1)}, bf16[128,8192]{1,0:T(8,128)(2,1)S(1)}, u32[]{:S(2)}) copy-start(bf16[128,8192]{1,0:T(8,128)(2,1)S(1)} %maximum_select_fusion.refs_0_) | copy-start | bytes 6291460
  5.2 27.1 %collective-permute-start.1 = (bf16[128,8192]{1,0:T(8,128)(2,1)S(1)}, bf16[128,8192]{1,0:T(8,128)(2,1)S(1)}, u32[]{:S(2)}, u32[]{:S(2)}) collective-permute-start(bf16[128,8192]{1,0:T(8,128)(2,1)S(1)} %maximum_select_fusion.refs_0_), channel_id=1, source_target_pairs={{0,4},{2,6},{4,8},{6,10},{8,12},{10,14},{5,1},{7,3},{9,5},{11,7},{... | collective-permute-start | bytes 6291464 | tf_op jit(solution)/shard_map/ppermute | solution.py:204
  32.3 48.3 %copy-start = (bf16[128,8192]{1,0:T(8,128)(2,1)}, bf16[128,8192]{1,0:T(8,128)(2,1)S(1)}, u32[]{:S(2)}) copy-start(bf16[128,8192]{1,0:T(8,128)(2,1)S(1)} %collective-permute-done.1.refs_0_) | copy-start | bytes 6291460
  32.3 26.9 %collective-permute-start.5 = (bf16[128,8192]{1,0:T(8,128)(2,1)S(1)}, bf16[128,8192]{1,0:T(8,128)(2,1)}, u32[]{:S(2)}, u32[]{:S(2)}) collective-permute-start(bf16[128,8192]{1,0:T(8,128)(2,1)S(1)} %collective-permute-done.1.refs_0_), channel_id=1, source_target_pairs={{4,8},{6,10},{8,12},{10,14},{5,1},{7,3},{9,5},{11,7},{20,24},{22,2... | collective-permute-start | bytes 6291464 | tf_op jit(solution)/shard_map/ppermute | solution.py:204
  59.2 57.7 %collective-permute-start.9 = (bf16[128,8192]{1,0:T(8,128)(2,1)}, bf16[128,8192]{1,0:T(8,128)(2,1)}, u32[]{:S(2)}, u32[]{:S(2)}) collective-permute-start(bf16[128,8192]{1,0:T(8,128)(2,1)} %collective-permute-done.5.refs_4_), channel_id=1, source_target_pairs={{8,12},{10,14},{5,1},{7,3},{24,28},{26,30},{21,17},{23,19}} | collective-permute-start | bytes 6291464 | tf_op jit(solution)/shard_map/ppermute | solution.py:204
  66.1 11.1 %copy-start.5 = (bf16[64,8192]{1,0:T(8,128)(2,1)S(1)}, bf16[64,8192]{1,0:T(8,128)(2,1)}, u32[]{:S(2)}) copy-start(bf16[64,8192]{1,0:T(8,128)(2,1)} %param.7) | copy-start | bytes 3145732
  66.1 129.6 %copy-start.9 = (s32[16]{0:T(128)S(1)}, s32[16]{0:T(128)}, u32[]{:S(2)}) copy-start(s32[16]{0:T(128)} %param.11) | copy-start | bytes 196
  66.1 129.7 %copy-start.8 = (s32[16]{0:T(128)S(1)}, s32[16]{0:T(128)}, u32[]{:S(2)}) copy-start(s32[16]{0:T(128)} %param.12) | copy-start | bytes 196
  66.1 237.2 %all-to-all-start.1 = ((bf16[16,64,1792]{2,1,0:T(8,128)(2,1)}), bf16[16,64,1792]{2,1,0:T(8,128)(2,1)}, u32[]{:S(2)}, u32[]{:S(2)}) async-start(bf16[16,64,1792]{2,1,0:T(8,128)(2,1)} %bitcast.31), calls=%async_computation.1 | async-start | bytes 7340032 | tf_op jit(solution)/shard_map/all_to_all | solution.py:207
  75.0 109.4 %collective-permute-start.2 = (bf16[128,8192]{1,0:T(8,128)(2,1)S(1)}, bf16[128,8192]{1,0:T(8,128)(2,1)}, u32[]{:S(2)}, u32[]{:S(2)}) collective-permute-start(bf16[128,8192]{1,0:T(8,128)(2,1)S(1)} %collective-permute-done.1.refs_0_), channel_id=1, source_target_pairs={{1,3},{3,1},{4,6},{5,7},{6,4},{7,5},{8,10},{9,11},{10,8},{11,9},{1... | collective-permute-start | bytes 6291464 | tf_op jit(solution)/shard_map/ppermute | solution.py:204
  77.2 105.9 %collective-permute-start.13 = (bf16[64,8192]{1,0:T(8,128)(2,1)S(1)}, bf16[64,8192]{1,0:T(8,128)(2,1)}, u32[]{:S(2)}, u32[]{:S(2)}) collective-permute-start(bf16[64,8192]{1,0:T(8,128)(2,1)S(1)} %copy-done.5), channel_id=1, source_target_pairs={{0,2},{1,3},{2,0},{3,1},{4,6},{5,7},{6,4},{7,5},{8,10},{9,11},{10,... | collective-permute-start | bytes 3145736 | tf_op jit(solution)/shard_map/ppermute | solution.py:204
  78.5 127.3 %collective-permute-start.6 = (bf16[128,8192]{1,0:T(8,128)(2,1)}, bf16[128,8192]{1,0:T(8,128)(2,1)}, u32[]{:S(2)}, u32[]{:S(2)}) collective-permute-start(bf16[128,8192]{1,0:T(8,128)(2,1)} %collective-permute-done.5.refs_4_), channel_id=1, source_target_pairs={{1,3},{3,1},{5,7},{7,5},{8,10},{10,8},{12,14},{14,12},{17,19},{19,... | collective-permute-start | bytes 6291464 | tf_op jit(solution)/shard_map/ppermute | solution.py:204
  80.7 136.8 %collective-permute-start.3 = (bf16[128,8192]{1,0:T(8,128)(2,1)S(1)}, bf16[128,8192]{1,0:T(8,128)(2,1)}, u32[]{:S(2)}, u32[]{:S(2)}) collective-permute-start(bf16[128,8192]{1,0:T(8,128)(2,1)S(1)} %collective-permute-done.1.refs_0_), channel_id=1, source_target_pairs={{1,0},{3,2},{4,5},{5,4},{6,7},{7,6},{8,9},{9,8},{10,11},{11,10},{1... | collective-permute-start | bytes 6291464 | tf_op jit(solution)/shard_map/ppermute | solution.py:204
  116.9 101.4 %collective-permute-start.10 = (bf16[128,8192]{1,0:T(8,128)(2,1)}, bf16[128,8192]{1,0:T(8,128)(2,1)}, u32[]{:S(2)}, u32[]{:S(2)}) collective-permute-start(bf16[128,8192]{1,0:T(8,128)(2,1)} %collective-permute-done.9.refs_8_), channel_id=1, source_target_pairs={{1,3},{3,1},{12,14},{14,12},{17,19},{19,17},{28,30},{30,28}} | collective-permute-start | bytes 6291464 | tf_op jit(solution)/shard_map/ppermute | solution.py:204
  183.1 14.0 %collective-permute-start.14 = (bf16[64,8192]{1,0:T(8,128)(2,1)}, bf16[64,8192]{1,0:T(8,128)(2,1)S(1)}, u32[]{:S(2)}, u32[]{:S(2)}) collective-permute-start(bf16[64,8192]{1,0:T(8,128)(2,1)} %collective-permute-done.13.refs_1_), channel_id=1, source_target_pairs={{0,1},{1,0},{2,3},{3,2},{4,5},{5,4},{6,7},{7,6},{8,9},{9,8},{10,11... | collective-permute-start | bytes 3145736 | tf_op jit(solution)/shard_map/ppermute | solution.py:204
  184.5 55.8 %collective-permute-start.4 = (bf16[128,8192]{1,0:T(8,128)(2,1)}, bf16[128,8192]{1,0:T(8,128)(2,1)}, u32[]{:S(2)}, u32[]{:S(2)}) collective-permute-start(bf16[128,8192]{1,0:T(8,128)(2,1)} %collective-permute-done.2.refs_1_), channel_id=1, source_target_pairs={{1,0},{3,2},{4,5},{5,4},{6,7},{7,6},{8,9},{9,8},{10,11},{11,10},{1... | collective-permute-start | bytes 6291464 | tf_op jit(solution)/shard_map/ppermute | solution.py:204
  197.1 22.1 %copy-start.6 = (bf16[64,8192]{1,0:T(8,128)(2,1)}, bf16[64,8192]{1,0:T(8,128)(2,1)S(1)}, u32[]{:S(2)}) copy-start(bf16[64,8192]{1,0:T(8,128)(2,1)S(1)} %collective-permute-done.14.refs_2_) | copy-start | bytes 3145732
  197.1 63.2 %collective-permute-start.7 = (bf16[128,8192]{1,0:T(8,128)(2,1)}, bf16[128,8192]{1,0:T(8,128)(2,1)}, u32[]{:S(2)}, u32[]{:S(2)}) collective-permute-start(bf16[128,8192]{1,0:T(8,128)(2,1)} %collective-permute-done.5.refs_4_), channel_id=1, source_target_pairs={{1,0},{3,2},{5,4},{7,6},{8,9},{10,11},{12,13},{14,15},{17,16},{19,... | collective-permute-start | bytes 6291464 | tf_op jit(solution)/shard_map/ppermute | solution.py:204
  205.8 54.6 %collective-permute-start.8 = (bf16[128,8192]{1,0:T(8,128)(2,1)}, bf16[128,8192]{1,0:T(8,128)(2,1)}, u32[]{:S(2)}, u32[]{:S(2)}) collective-permute-start(bf16[128,8192]{1,0:T(8,128)(2,1)} %collective-permute-done.6.refs_5_), channel_id=1, source_target_pairs={{1,0},{3,2},{5,4},{7,6},{8,9},{10,11},{12,13},{14,15},{17,16},{19,... | collective-permute-start | bytes 6291464 | tf_op jit(solution)/shard_map/ppermute | solution.py:204
  208.4 31.9 %copy-start.7 = (s32[16]{0:T(128)}, s32[16]{0:T(128)S(1)}, u32[]{:S(2)}) copy-start(s32[16]{0:T(128)S(1)} %broadcast_minimum_fusion.begins) | copy-start | bytes 196
  217.5 62.9 %collective-permute-start.11 = (bf16[128,8192]{1,0:T(8,128)(2,1)}, bf16[128,8192]{1,0:T(8,128)(2,1)S(1)}, u32[]{:S(2)}, u32[]{:S(2)}) collective-permute-start(bf16[128,8192]{1,0:T(8,128)(2,1)} %collective-permute-done.9.refs_8_), channel_id=1, source_target_pairs={{1,0},{3,2},{12,13},{14,15},{17,16},{19,18},{28,29},{30,31}} | collective-permute-start | bytes 6291464 | tf_op jit(solution)/shard_map/ppermute | solution.py:204
  218.3 62.1 %collective-permute-start.12 = (bf16[128,8192]{1,0:T(8,128)(2,1)}, bf16[128,8192]{1,0:T(8,128)(2,1)S(1)}, u32[]{:S(2)}, u32[]{:S(2)}) collective-permute-start(bf16[128,8192]{1,0:T(8,128)(2,1)} %collective-permute-done.10.refs_9_), channel_id=1, source_target_pairs={{1,0},{3,2},{12,13},{14,15},{17,16},{19,18},{28,29},{30,31}} | collective-permute-start | bytes 6291464 | tf_op jit(solution)/shard_map/ppermute | solution.py:204
  280.4 1.3 copy-start.3
  280.4 2.0 copy-start.4

commit v2 on v0

v2 whole, which is shorter than its diff:
```python
import functools

import jax
import jax.numpy as jnp
from jax import lax
from jax.experimental import pallas as pl
from jax.experimental.pallas import tpu as pltpu
from jax.sharding import PartitionSpec as P

BLOCK = 32
MOST = 4
AXIS = "tensor"
VMEM_LIMIT = 56 * 1024 * 1024
ANY = pl.BlockSpec(memory_space=pltpu.HBM)


def tie(values, after):
    count = len(values)

    def body(*refs):
        del refs

    return pl.pallas_call(
        body,
        out_shape=[jax.ShapeDtypeStruct(v.shape, v.dtype) for v in values],
        in_specs=[ANY] * (count + len(after)),
        out_specs=[ANY] * count,
        input_output_aliases={i: i for i in range(count)},
        name="tie",
    )(*values, *after)


def order(values, after):
    return lax.optimization_barrier(tuple(values) + tuple(after))[: len(values)]


def chips_kernel(heights, scalars, *refs):
    count = len(heights)
    pieces = refs[:count]
    weight, shrink_t = refs[count : count + 2]
    out, shrunk, rows, narrow, sem, narrow_sem = refs[-6:]

    def narrow_copies():
        copies = []
        at = 0
        for i, height in enumerate(heights):
            copies.append(
                pltpu.make_async_copy(
                    narrow.at[pl.ds(at, height)],
                    shrunk.at[pl.ds(pl.multiple_of(scalars[i], height), height)],
                    narrow_sem.at[i],
                )
            )
            at += height
        return copies

    @pl.when(pl.program_id(0) == 0)
    def _():
        copies = []
        at = 0
        for i, height in enumerate(heights):
            copies.append(pltpu.make_async_copy(pieces[i], rows.at[pl.ds(at, height)], sem.at[i]))
            copies[-1].start()
            at += height
        for copy in copies:
            copy.wait()
        s = lax.dot_general(
            rows[...], shrink_t[...], (((1,), (1,)), ((), ())), preferred_element_type=jnp.float32
        ).astype(narrow.dtype)
        narrow[...] = jnp.concatenate([s, jnp.zeros_like(s)], axis=1)
        for copy in narrow_copies():
            copy.start()

    out[...] = jnp.dot(rows[...], weight[...], preferred_element_type=jnp.float32)

    @pl.when(pl.program_id(0) == pl.num_programs(0) - 1)
    def _():
        for copy in narrow_copies():
            copy.wait()


def chips_matmul(places, pieces, weight, shrink_t, held, total_rows, after, tile=256):
    depth, columns = weight.shape
    rank = shrink_t.shape[0]
    count = len(pieces)
    heights = [p.shape[0] for p in pieces]
    rows = sum(heights)
    while columns % tile:
        tile //= 2
    extra = ([] if held is None else [held]) + list(after)
    return pl.pallas_call(
        functools.partial(chips_kernel, heights),
        out_shape=[
            jax.ShapeDtypeStruct((rows, columns), jnp.float32),
            jax.ShapeDtypeStruct((total_rows, 2 * rank), jnp.bfloat16),
        ],
        grid_spec=pltpu.PrefetchScalarGridSpec(
            num_scalar_prefetch=1,
            grid=(columns // tile,),
            in_specs=[ANY] * count
            + [
                pl.BlockSpec((depth, tile), lambda n, s: (0, n)),
                pl.BlockSpec((rank, depth), lambda n, s: (0, 0)),
            ]
            + [ANY] * len(extra),
            out_specs=[pl.BlockSpec((rows, tile), lambda n, s: (0, n)), ANY],
            scratch_shapes=[
                pltpu.VMEM((rows, depth), jnp.bfloat16),
                pltpu.VMEM((rows, 2 * rank), jnp.bfloat16),
                pltpu.SemaphoreType.DMA((count,)),
                pltpu.SemaphoreType.DMA((count,)),
            ],
        ),
        input_output_aliases={} if held is None else {3 + count: 1},
        compiler_params=pltpu.CompilerParams(vmem_limit_bytes=VMEM_LIMIT),
        cost_estimate=pl.CostEstimate(
            flops=2 * rows * depth * columns,
            bytes_accessed=2 * depth * columns + 2 * rows * depth + 4 * rows * columns,
            transcendentals=0,
        ),
        name="chips",
    )(jnp.stack(places).astype(jnp.int32), *pieces, weight, shrink_t, *extra)


def spread_kernel(slots, rank, begins, shrunk, spread):
    capacity = shrunk.shape[0] // slots
    spread[...] = jnp.zeros_like(spread)
    for s in range(slots):
        rows = pl.ds(pl.multiple_of(begins[s], BLOCK), capacity)
        spread[rows, s * rank : (s + 1) * rank] = shrunk[s * capacity : (s + 1) * capacity, :rank]


def spread_rows(begins, shrunk, total_rows, rank):
    slots = begins.shape[0]
    return pl.pallas_call(
        functools.partial(spread_kernel, slots, rank),
        out_shape=jax.ShapeDtypeStruct((total_rows, slots * rank), jnp.bfloat16),
        in_specs=[pl.BlockSpec(memory_space=pltpu.SMEM), pl.BlockSpec(memory_space=pltpu.VMEM)],
        out_specs=pl.BlockSpec(memory_space=pltpu.VMEM),
        compiler_params=pltpu.CompilerParams(vmem_limit_bytes=VMEM_LIMIT),
        name="spread",
    )(begins, shrunk)


def last_kernel(parts, scalars, *refs):
    bases = refs[: len(parts)]
    spread, expand, out = refs[len(parts) :]
    i = 0
    for base, heights in zip(bases, parts):
        at = 0
        for height in heights:
            rows = pl.ds(pl.multiple_of(scalars[i], height), height)
            lora = jnp.dot(spread[rows, :], expand[...], preferred_element_type=jnp.float32).astype(jnp.bfloat16)
            out[rows, :] = (base[at : at + height] + lora.astype(jnp.float32)).astype(jnp.bfloat16)
            at += height
            i += 1


def last(places, parts, bases, spread, expand, tile=256):
    total_rows = spread.shape[0]
    inner, columns = expand.shape
    while columns % tile:
        tile //= 2
    return pl.pallas_call(
        functools.partial(last_kernel, parts),
        out_shape=jax.ShapeDtypeStruct((total_rows, columns), jnp.bfloat16),
        grid_spec=pltpu.PrefetchScalarGridSpec(
            num_scalar_prefetch=1,
            grid=(columns // tile,),
            in_specs=[pl.BlockSpec((base.shape[0], tile), lambda n, s: (0, n)) for base in bases]
            + [
                pl.BlockSpec((total_rows, inner), lambda n, s: (0, 0)),
                pl.BlockSpec((inner, tile), lambda n, s: (0, n)),
            ],
            out_specs=pl.BlockSpec((total_rows, tile), lambda n, s: (0, n)),
        ),
        compiler_params=pltpu.CompilerParams(vmem_limit_bytes=VMEM_LIMIT),
        cost_estimate=pl.CostEstimate(
            flops=2 * total_rows * inner * columns,
            bytes_accessed=6 * total_rows * columns + 2 * inner * columns,
            transcendentals=0,
        ),
        name="last",
    )(jnp.stack(places).astype(jnp.int32), *bases, spread, expand)


def local(tokens, gate_weight, adapter_shrink, adapter_expand, adapter_blocks, adapter_position):
    width = lax.axis_size(AXIS)
    me = lax.axis_index(AXIS)
    shard, depth = tokens.shape
    columns = gate_weight.shape[1]
    rank = adapter_shrink.shape[2]
    total_rows = shard * width
    chips = width // 2
    chip_rows = 2 * shard
    chip, core = me // 2, me % 2

    count = adapter_position.shape[0]
    ids = jnp.arange(count, dtype=jnp.int32)
    capacity = MOST * BLOCK
    starts = jnp.sum(jnp.where(ids[None, :] < ids[:, None], adapter_blocks[None, :], 0), axis=1) * BLOCK
    sizes = adapter_blocks * BLOCK
    at_slot = adapter_position[None, :] == ids[:, None]
    start_by_slot = jnp.sum(jnp.where(at_slot, starts[None, :], 0), axis=1)
    size_by_slot = jnp.sum(jnp.where(at_slot, sizes[None, :], 0), axis=1)
    begin_by_slot = jnp.minimum(start_by_slot, total_rows - capacity)

    ring = list(range(0, chips, 2)) + list(range(chips - 1, 0, -2))
    place = [ring.index(a) for a in range(chips)]
    swap_core = [(a * 2 + c, a * 2 + 1 - c) for a in range(chips) for c in range(2)]
    around = [
        (a * 2 + c, ring[(place[a] + 1 - 2 * c) % chips] * 2 + c) for a in range(chips) for c in range(2)
    ]
    behind = jnp.asarray([[ring[(place[a] - j) % chips] for j in range(chips)] for a in range(chips)], jnp.int32)
    behind = lax.dynamic_index_in_dim(behind, chip, 0, keepdims=False)

    def send(value, pairs):
        return lax.ppermute(value, AXIS, pairs)

    shrink_t = jnp.swapaxes(adapter_shrink[0], 0, 1)
    expand_parts = adapter_expand.reshape(rank, width, columns).transpose(1, 0, 2)

    neighbour = send(tokens, swap_core)
    whole = jnp.where(core == 0, jnp.concatenate([tokens, neighbour]), jnp.concatenate([neighbour, tokens]))
    half_way = chips // 2
    carried = send(whole, around)
    pieces, places = [whole], [chip * chip_rows]
    bases, parts, all_places, shrunk = [], [], [], None
    for j in range(1, half_way + 1):
        onward = None
        if j >= 2 and j < half_way:
            carried = order([carried], [shrunk])[0]
        if j + 1 < half_way:
            onward = send(carried, around)
        elif j + 1 == half_way:
            half = jnp.where(core == 0, carried[:shard], carried[shard:])
            onward = send(half, around)
        swapped = send(carried, swap_core)
        mine_from = jnp.where(core == 0, behind[j], behind[chips - j]) * chip_rows
        other_from = jnp.where(core == 0, behind[chips - j], behind[j]) * chip_rows
        if j == half_way:
            mine_from, other_from = mine_from + core * shard, other_from + (1 - core) * shard
            (expand_parts,) = order([expand_parts], [carried, previous])
            expand = lax.all_to_all(expand_parts, AXIS, split_axis=0, concat_axis=0, tiled=True)
        pieces += [carried, swapped]
        places += [mine_from, other_from]
        if j + 1 != half_way:
            base, shrunk = chips_matmul(
                places, pieces, gate_weight, shrink_t, shrunk, total_rows, [] if onward is None else [carried]
            )
            bases.append(base)
            parts.append([p.shape[0] for p in pieces])
            all_places += places
            pieces, places = [], []
        carried, previous = onward, swapped

    my_begin, my_start, my_size = begin_by_slot[me], start_by_slot[me], size_by_slot[me]
    rows = my_begin + jnp.arange(capacity, dtype=jnp.int32)
    keep = (rows >= my_start) & (rows < my_start + my_size)
    chosen = lax.dynamic_slice_in_dim(shrunk, my_begin, capacity, 0)
    chosen = jnp.where(keep[:, None], chosen, jnp.zeros_like(chosen))
    shrunk_all = lax.all_gather(chosen, AXIS, axis=0, tiled=True)
    spread = spread_rows(begin_by_slot.astype(jnp.int32), shrunk_all, total_rows, rank)
    return last(all_places, parts, bases, spread, expand.reshape(width * rank, columns))


def solution(mesh):
    return jax.shard_map(
        local,
        mesh=mesh,
        in_specs=(
            P(("groups", "tensor"), None),
            P(None, "tensor"),
            P(("groups", "tensor"), None, None),
            P(("groups", "tensor"), None, None),
            P("groups"),
            P("groups"),
        ),
        out_specs=P("groups", "tensor"),
        check_vma=False,
    )
```

time: 394 us -> 221 us (0.56)
  waiting for transfers between devices: 282 us -> 35.8 us
  Pallas kernels: 0 us -> 81.5 us
  blocking collectives: 0 us -> 57.1 us
  matrix products: 52.9 us -> 0 us
  other arithmetic: 30.9 us -> 7.93 us
  starting transfers between devices: 7.74 us -> 14.8 us
  local copies, waits for them, and re-layouts: 4.77 us -> 9.99 us
    all_to_all x1, waiting for transfers between devices: 160 us -> 0.01 us  [local(): lax.all_to_all(expand_parts, AXIS, split_axis=0, concat_axis=0, tiled=True)]
    all_gather x1 -> x0, waiting for transfers between devices: 122 us -> none  [local(): piece = lax.all_gather(tokens, 'tensor', axis=0, tiled=True)]
    pallas_call x0 -> x5, Pallas kernels: none -> 81.5 us  [the longest x3 67.2 us: chips_matmul(): pl.pallas_call(functools.partial(chips_kernel, heights), out_shape=[jax.S...]
    all_gather x0 -> x1, blocking collectives: none -> 57.1 us  [local(): shrunk_all = lax.all_gather(chosen, AXIS, axis=0, tiled=True)]
    dot_general x3 -> x0, matrix products: 52.9 us -> none  [the longest x1 39.6 us: local(): base_part = jnp.dot(piece, gate_weight, preferred_element_type=jnp.float32)]
    ppermute x0 -> x9, waiting for transfers between devices: none -> 35.8 us  [send(): return lax.ppermute(value, AXIS, pairs)]
    scatter-add x1 -> x0, other arithmetic: 27.8 us -> none  [local(): adapter_output = jnp.zeros((gathered_rows, column_width), jnp.bfloat16).a...]
    ppermute x0 -> x9, starting transfers between devices: none -> 9.05 us  [send(): return lax.ppermute(value, AXIS, pairs)]
  transfers between devices with their start and end apart: 2 -> 10, of which waited for: 2 -> 4; matrix products, arithmetic and copies ran while one was open for 1% -> 6% of each run, Pallas kernels for 0% -> 32%
where the time goes in v2:
time: 221 us; the launch traced here: 219 us
  Pallas kernels  81.5 us (37%)
  blocking collectives  57.1 us (26%)
  waiting for transfers between devices  35.8 us (16%)
  starting transfers between devices  14.8 us (7%)
  between operations  11.6 us (5%)
  local copies, waits for them, and re-layouts  9.99 us (5%)
  other arithmetic  7.93 us (4%)
    pallas_call x3, Pallas kernels, chips_matmul(): pl.pallas_call(functools.partial(chips_kernel, heights), out_shape=[jax.S...  67.2 us
    all_gather x1, blocking collectives, local(): shrunk_all = lax.all_gather(chosen, AXIS, axis=0, tiled=True)  57.1 us
    ppermute x9, waiting for transfers between devices, send(): return lax.ppermute(value, AXIS, pairs)  35.8 us
    pallas_call x1, Pallas kernels, last(): pl.pallas_call(functools.partial(last_kernel, parts), out_shape=jax.Shape...  11.6 us
    ppermute x9, starting transfers between devices, send(): return lax.ppermute(value, AXIS, pairs)  9.05 us
    all_to_all x1, starting transfers between devices, local(): lax.all_to_all(expand_parts, AXIS, split_axis=0, concat_axis=0, tiled=True)  5.73 us
  transfers between devices with their start and end apart: 10, of which 4 were waited for; matrix products, arithmetic and copies ran while one was open for 6% of the time, Pallas kernels for 32%

profile of v2, /device:TPU:13, one launch (start us, length us, event | category | flops | bytes accessed | tf_op | source)
XLA Modules:
  0.0 218.7 jit_solution(16918560639741979090)
XLA Ops:
  0.0 0.7 collective-permute-start
  0.7 2.5 %collective-permute-done = bf16[64,8192]{1,0:T(8,128)(2,1)S(1)} collective-permute-done((bf16[64,8192]{1,0:T(8,128)(2,1)}, bf16[64,8192]{1,0:T(8,128)(2,1)S(1)}, u32[]{:S(2)}, u32[]{:S(2)}) %collective-permute-start) | collective-permute-done | bytes 1048608 | tf_op jit(solution)/shard_map/ppermute | solution.py:218
  3.2 2.0 maximum_select_fusion.refs_0_
  5.2 1.3 collective-permute-start.1
  6.6 24.0 %collective-permute-done.1.refs_1_.refs_5_ = bf16[128,8192]{1,0:T(8,128)(2,1)} collective-permute-done((bf16[128,8192]{1,0:T(8,128)(2,1)S(1)}, bf16[128,8192]{1,0:T(8,128)(2,1)}, u32[]{:S(2)}, u32[]{:S(2)}) %collective-permute-start.1) | collective-permute-done | bytes 2097184 | tf_op jit(solution)/shard_map/ppermute | solution.py:218
  30.5 1.2 collective-permute-start.2
  31.8 1.3 collective-permute-start.3
  33.1 0.7 constant_dynamic-slice_fusion
  33.8 0.7 fusion
  37.1 0.7 pad_add_fusion.scalars
  37.8 23.4 %chips.3 = (f32[384,1792]{1,0:T(8,128)}, bf16[1024,128]{1,0:T(8,128)(2,1)}) custom-call(s32[3]{0:T(128)} %pad_add_fusion.scalars, bf16[128,8192]{1,0:T(8,128)(2,1)} %copy-done.2, bf16[128,8192]{1,0:T(8,128)(2,1)} %collective-permute-done.1.refs_1_.refs_5_, bf16[128,8192]{1,0:T(8,128)(2,1)} %collective-permute-done.2.refs_2_, bf16[8192,1792]{1,0:T(8,128)(2,1)} %refs_4_.1, ...), custom_call_target="tpu_custom_call" | custom-call | flops 11274289152 | bytes 38404096 | tf_op jit(solution)/shard_map/chips/pallas_call | solution.py:91
  61.3 1.4 collective-permute-start.5
  65.7 20.5 %chips.4 = (f32[256,1792]{1,0:T(8,128)}, bf16[1024,128]{1,0:T(8,128)(2,1)}) custom-call(s32[2]{0:T(128)} %pad_add_fusion.1.scalars, bf16[128,8192]{1,0:T(8,128)(2,1)} %copy-done, bf16[128,8192]{1,0:T(8,128)(2,1)} %collective-permute-done.4.refs_1_, bf16[8192,1792]{1,0:T(8,128)(2,1)} %refs_4_.1, ...), custom_call_target="tpu_custom_call", output_to_operand_aliasing={{1}: (5, {})} | custom-call | flops 7516192768 | bytes 35389440 | tf_op jit(solution)/shard_map/chips/pallas_call | solution.py:91
  86.6 1.3 collective-permute-start.6
  87.9 1.7 slice_select_fusion
  89.5 1.4 collective-permute-start.7
  90.9 0.7 copy.12
  91.6 2.9 %copy.14 = bf16[64,16,1792]{2,0,1:T(8,128)(2,1)} copy(bf16[64,16,1792]{2,1,0:T(8,128)(2,1)S(1)} %bitcast.30) | data formatting | bytes 7340032 | tf_op jit(solution)/shard_map/reshape | solution.py:221
  94.6 9.0 %collective-permute-done.7.refs_2_ = bf16[64,8192]{1,0:T(8,128)(2,1)S(1)} collective-permute-done((bf16[64,8192]{1,0:T(8,128)(2,1)S(1)}, bf16[64,8192]{1,0:T(8,128)(2,1)S(1)}, u32[]{:S(2)}, u32[]{:S(2)}) %collective-permute-start.7) | collective-permute-done | bytes 1048608 | tf_op jit(solution)/shard_map/ppermute | solution.py:218
  103.6 1.4 copy-done.6
  105.0 5.7 %all-to-all-start = ((bf16[16,64,1792]{2,1,0:T(8,128)(2,1)}), bf16[16,64,1792]{2,1,0:T(8,128)(2,1)}, u32[]{:S(2)}, u32[]{:S(2)}) async-start(bf16[16,64,1792]{2,1,0:T(8,128)(2,1)} %bitcast.29), calls=%async_computation | async-start | bytes 7340032 | tf_op jit(solution)/shard_map/all_to_all | solution.py:244
  114.5 0.6 dynamic_slice.18
  115.1 0.6 dynamic_slice.19
  119.5 0.7 stack.57.scalars
  120.2 0.7 pad_add_fusion.2.scalars
  120.9 1.3 compare_and_fusion
  122.2 1.0 copy-done.8
  123.1 23.4 %chips.5 = (f32[384,1792]{1,0:T(8,128)}, bf16[1024,128]{1,0:T(8,128)(2,1)}) custom-call(s32[4]{0:T(128)} %pad_add_fusion.2.scalars, bf16[128,8192]{1,0:T(8,128)(2,1)} %collective-permute-done.5.refs_0_, bf16[128,8192]{1,0:T(8,128)(2,1)} %copy-done.6, bf16[64,8192]{1,0:T(8,128)(2,1)} %copy-done.7, ...), custom_call_target="tpu_custom_call", output_to_operand_aliasing={{1}: (7, {})} | custom-call | flops 11274289152 | bytes 38404096 | tf_op jit(solution)/shard_map/chips/pallas_call | solution.py:91
  146.5 0.9 dynamic-slice_select_fusion
  147.4 57.1 %all_gather.3.shrunk = bf16[2048,128]{1,0:T(8,128)(2,1)} all-gather(bf16[128,128]{1,0:T(8,128)(2,1)S(1)} %dynamic-slice_select_fusion), channel_id=1, replica_groups=mesh['groups'=2,'tensor'=16] {'tensor'}, dimensions={0}, use_global_device_ids=true | all-gather | bytes 557056 | tf_op jit(solution)/shard_map/all_gather | solution.py:262
  204.4 2.7 %spread.1.refs_3_ = bf16[1024,1024]{1,0:T(8,128)(2,1)} custom-call(s32[16]{0:T(128)} %copy-done.5, bf16[2048,128]{1,0:T(8,128)(2,1)} %all_gather.3.shrunk), custom_call_target="tpu_custom_call" | custom-call | tf_op jit(solution)/shard_map/spread/pallas_call | solution.py:135
  207.1 11.6 %last.1 = bf16[1024,1792]{1,0:T(8,128)(2,1)} custom-call(s32[9]{0:T(128)} %stack.57.scalars, f32[384,1792]{1,0:T(8,128)} %get-tuple-element.14.refs_0_, f32[256,1792]{1,0:T(8,128)} %get-tuple-element.17.refs_1_, f32[384,1792]{1,0:T(8,128)} %get-tuple-element.20.refs_2_, bf16[1024,1024]{1,0:T(8,128)(2,1)} %spread.1.refs_3_, bf16[1024,1792]{1,0:T(8,128)(2,1)} %bitcast.23.refs_4_), custom_call_target="tpu_custom_call" | custom-call | flops 3758096384 | bytes 14680064 | tf_op jit(solution)/shard_map/last/pallas_call | solution.py:164
  (31 shorter events, 2.4 us)
Async XLA Ops:
  0.0 3.2 %collective-permute-start = (bf16[64,8192]{1,0:T(8,128)(2,1)}, bf16[64,8192]{1,0:T(8,128)(2,1)S(1)}, u32[]{:S(2)}, u32[]{:S(2)}) collective-permute-start(bf16[64,8192]{1,0:T(8,128)(2,1)} %param.7), channel_id=1, source_target_pairs={{0,1},{1,0},{2,3},{3,2},{4,5},{5,4},{6,7},{7,6},{8,9},{9,8},{10,11... | collective-permute-start | bytes 3145736 | tf_op jit(solution)/shard_map/ppermute | solution.py:218
  5.2 25.4 %copy-start.2 = (bf16[128,8192]{1,0:T(8,128)(2,1)}, bf16[128,8192]{1,0:T(8,128)(2,1)S(1)}, u32[]{:S(2)}) copy-start(bf16[128,8192]{1,0:T(8,128)(2,1)S(1)} %maximum_select_fusion.refs_0_) | copy-start | bytes 6291460
  5.2 25.3 %collective-permute-start.1 = (bf16[128,8192]{1,0:T(8,128)(2,1)S(1)}, bf16[128,8192]{1,0:T(8,128)(2,1)}, u32[]{:S(2)}, u32[]{:S(2)}) collective-permute-start(bf16[128,8192]{1,0:T(8,128)(2,1)S(1)} %maximum_select_fusion.refs_0_), channel_id=1, source_target_pairs={{0,4},{1,3},{2,0},{3,7},{4,8},{5,1},{6,2},{7,11},{8,12},{9,5},{10,... | collective-permute-start | bytes 6291464 | tf_op jit(solution)/shard_map/ppermute | solution.py:218
  30.5 7.2 %collective-permute-start.2 = (bf16[128,8192]{1,0:T(8,128)(2,1)}, bf16[128,8192]{1,0:T(8,128)(2,1)}, u32[]{:S(2)}, u32[]{:S(2)}) collective-permute-start(bf16[128,8192]{1,0:T(8,128)(2,1)} %collective-permute-done.1.refs_1_.refs_5_), channel_id=1, source_target_pairs={{0,1},{1,0},{2,3},{3,2},{4,5},{5,4},{6,7},{7,6},{8,9},{9,8},{10,11... | collective-permute-start | bytes 6291464 | tf_op jit(solution)/shard_map/ppermute | solution.py:218
  31.8 29.4 %collective-permute-start.3 = (bf16[128,8192]{1,0:T(8,128)(2,1)}, bf16[128,8192]{1,0:T(8,128)(2,1)S(1)}, u32[]{:S(2)}, u32[]{:S(2)}) collective-permute-start(bf16[128,8192]{1,0:T(8,128)(2,1)} %collective-permute-done.1.refs_1_.refs_5_), channel_id=1, source_target_pairs={{0,4},{1,3},{2,0},{3,7},{4,8},{5,1},{6,2},{7,11},{8,12},{9,5},{10,... | collective-permute-start | bytes 6291464 | tf_op jit(solution)/shard_map/ppermute | solution.py:218
  61.2 4.6 %copy-start = (bf16[128,8192]{1,0:T(8,128)(2,1)}, bf16[128,8192]{1,0:T(8,128)(2,1)S(1)}, u32[]{:S(2)}) copy-start(bf16[128,8192]{1,0:T(8,128)(2,1)S(1)} %collective-permute-done.3.refs_0_.refs_5_) | copy-start | bytes 6291460
  61.2 4.6 %collective-permute-start.4 = (bf16[128,8192]{1,0:T(8,128)(2,1)S(1)}, bf16[128,8192]{1,0:T(8,128)(2,1)}, u32[]{:S(2)}, u32[]{:S(2)}) collective-permute-start(bf16[128,8192]{1,0:T(8,128)(2,1)S(1)} %collective-permute-done.3.refs_0_.refs_5_), channel_id=1, source_target_pairs={{0,1},{1,0},{2,3},{3,2},{4,5},{5,4},{6,7},{7,6},{8,9},{9,8},{10,11... | collective-permute-start | bytes 6291464 | tf_op jit(solution)/shard_map/ppermute | solution.py:218
  61.3 25.3 %collective-permute-start.5 = (bf16[128,8192]{1,0:T(8,128)(2,1)S(1)}, bf16[128,8192]{1,0:T(8,128)(2,1)}, u32[]{:S(2)}, u32[]{:S(2)}) collective-permute-start(bf16[128,8192]{1,0:T(8,128)(2,1)S(1)} %collective-permute-done.3.refs_0_.refs_5_), channel_id=1, source_target_pairs={{0,4},{1,3},{2,0},{3,7},{4,8},{5,1},{6,2},{7,11},{8,12},{9,5},{10,... | collective-permute-start | bytes 6291464 | tf_op jit(solution)/shard_map/ppermute | solution.py:218
  65.7 25.2 %copy-start.1 = (bf16[1,64,28672]{2,1,0:T(8,128)(2,1)S(1)}, bf16[1,64,28672]{2,1,0:T(8,128)(2,1)}, u32[]{:S(2)}) copy-start(bf16[1,64,28672]{2,1,0:T(8,128)(2,1)} %param.10) | copy-start | bytes 11010052
  86.6 17.0 %collective-permute-start.6 = (bf16[128,8192]{1,0:T(8,128)(2,1)}, bf16[128,8192]{1,0:T(8,128)(2,1)S(1)}, u32[]{:S(2)}, u32[]{:S(2)}) collective-permute-start(bf16[128,8192]{1,0:T(8,128)(2,1)} %collective-permute-done.5.refs_0_), channel_id=1, source_target_pairs={{0,1},{1,0},{2,3},{3,2},{4,5},{5,4},{6,7},{7,6},{8,9},{9,8},{10,11... | collective-permute-start | bytes 6291464 | tf_op jit(solution)/shard_map/ppermute | solution.py:218
  89.5 14.0 %collective-permute-start.7 = (bf16[64,8192]{1,0:T(8,128)(2,1)S(1)}, bf16[64,8192]{1,0:T(8,128)(2,1)S(1)}, u32[]{:S(2)}, u32[]{:S(2)}) collective-permute-start(bf16[64,8192]{1,0:T(8,128)(2,1)S(1)} %slice_select_fusion), channel_id=1, source_target_pairs={{0,4},{1,3},{2,0},{3,7},{4,8},{5,1},{6,2},{7,11},{8,12},{9,5},{10,... | collective-permute-start | bytes 3145736 | tf_op jit(solution)/shard_map/ppermute | solution.py:218
  103.5 7.2 %copy-start.7 = (bf16[64,8192]{1,0:T(8,128)(2,1)}, bf16[64,8192]{1,0:T(8,128)(2,1)S(1)}, u32[]{:S(2)}) copy-start(bf16[64,8192]{1,0:T(8,128)(2,1)S(1)} %collective-permute-done.7.refs_2_) | copy-start | bytes 3145732
  103.6 1.4 copy-start.6
  103.6 10.7 %copy-start.4 = (s32[16]{0:T(128)S(1)}, s32[16]{0:T(128)}, u32[]{:S(2)}) copy-start(s32[16]{0:T(128)} %param.11) | copy-start | bytes 196
  103.6 10.8 %copy-start.3 = (s32[16]{0:T(128)S(1)}, s32[16]{0:T(128)}, u32[]{:S(2)}) copy-start(s32[16]{0:T(128)} %param.12) | copy-start | bytes 196
  105.0 102.1 %all-to-all-start = ((bf16[16,64,1792]{2,1,0:T(8,128)(2,1)}), bf16[16,64,1792]{2,1,0:T(8,128)(2,1)}, u32[]{:S(2)}, u32[]{:S(2)}) async-start(bf16[16,64,1792]{2,1,0:T(8,128)(2,1)} %bitcast.29), calls=%async_computation | async-start | bytes 7340032 | tf_op jit(solution)/shard_map/all_to_all | solution.py:244
  110.7 11.4 %collective-permute-start.8 = (bf16[64,8192]{1,0:T(8,128)(2,1)S(1)}, bf16[64,8192]{1,0:T(8,128)(2,1)S(1)}, u32[]{:S(2)}, u32[]{:S(2)}) collective-permute-start(bf16[64,8192]{1,0:T(8,128)(2,1)S(1)} %collective-permute-done.7.refs_2_), channel_id=1, source_target_pairs={{0,1},{1,0},{2,3},{3,2},{4,5},{5,4},{6,7},{7,6},{8,9},{9,8},{10,11... | collective-permute-start | bytes 3145736 | tf_op jit(solution)/shard_map/ppermute | solution.py:218
  115.8 30.7 %copy-start.5 = (s32[16]{0:T(128)}, s32[16]{0:T(128)S(1)}, u32[]{:S(2)}) copy-start(s32[16]{0:T(128)S(1)} %broadcast_minimum_fusion.begins) | copy-start | bytes 196
  122.2 1.0 copy-start.8

commit v3 on v0

v3 whole, which is shorter than its diff:
```python
import functools

import jax
import jax.numpy as jnp
from jax import lax
from jax.experimental import pallas as pl
from jax.experimental.pallas import tpu as pltpu
from jax.sharding import PartitionSpec as P

BLOCK = 32
MOST = 4
AXIS = "tensor"
VMEM_LIMIT = 56 * 1024 * 1024
LANES = 128
ANY = pl.BlockSpec(memory_space=pltpu.HBM)


def order(values, after):
    return lax.optimization_barrier(tuple(values) + tuple(after))[: len(values)]


def parts_kernel(expand, low, high):
    count, tiles, height = low.shape[0], low.shape[1], low.shape[2]
    spare = high.shape[1] - tiles
    for i in range(count):
        for t in range(tiles):
            columns = expand[:, (i * tiles + t) * LANES : (i * tiles + t + 1) * LANES]
            low[i, t] = columns[:height]
            high[i, spare + t] = columns[height:]


def parts_of(expand, height, width, spare):
    rank, columns = expand.shape[0], expand.shape[1] // width
    tiles = columns // LANES
    return pl.pallas_call(
        parts_kernel,
        out_shape=[
            jax.ShapeDtypeStruct((width, tiles, height, LANES), expand.dtype),
            jax.ShapeDtypeStruct((width, tiles + spare, rank - height, LANES), expand.dtype),
        ],
        grid=(width // 4,),
        in_specs=[pl.BlockSpec((rank, 4 * columns), lambda d: (0, d))],
        out_specs=[
            pl.BlockSpec((4, tiles, height, LANES), lambda d: (d, 0, 0, 0)),
            pl.BlockSpec((4, tiles + spare, rank - height, LANES), lambda d: (d, 0, 0, 0)),
        ],
        compiler_params=pltpu.CompilerParams(vmem_limit_bytes=VMEM_LIMIT),
        cost_estimate=pl.CostEstimate(flops=0, bytes_accessed=4 * rank * columns * width, transcendentals=0),
        name="parts",
    )(expand)


def shrink_kernel(count, scalars, *refs):
    pieces = refs[:count]
    shrink_t, _, out, rows, packed, sem, out_sem = refs[count:]
    shard = pieces[0].shape[0]
    begin, start, size = scalars[count], scalars[count + 1], scalars[count + 2]

    for b in range(MOST):
        first = begin + b * BLOCK
        inside = lax.rem(first, shard)

        for i in range(count):

            @pl.when(scalars[i] == first - inside)
            def _():
                pltpu.make_async_copy(
                    pieces[i].at[pl.ds(pl.multiple_of(inside, BLOCK), BLOCK)],
                    rows.at[pl.ds(b * BLOCK, BLOCK)],
                    sem.at[b],
                ).start()

    for b in range(MOST):
        pltpu.make_async_copy(
            pieces[0].at[pl.ds(0, BLOCK)], rows.at[pl.ds(b * BLOCK, BLOCK)], sem.at[b]
        ).wait()

    s = lax.dot_general(rows[...], shrink_t[...], (((1,), (1,)), ((), ())), preferred_element_type=jnp.float32)
    row = begin + lax.broadcasted_iota(jnp.int32, s.shape, 0)
    s = jnp.where((row >= start) & (row < start + size), s, 0.0).astype(out.dtype)
    spare, height = packed.shape[0], packed.shape[1]
    half = MOST * BLOCK // 2
    both = jnp.concatenate([s[:half], s[half:]], axis=1)
    for i in range(spare):
        some = both[i * height : (i + 1) * height]
        packed[i, : some.shape[0]] = some
    copies = [
        pltpu.make_async_copy(packed, out.at[d, pl.ds(0, spare)], out_sem.at[d]) for d in range(out.shape[0])
    ]
    for copy in copies:
        copy.start()
    for copy in copies:
        copy.wait()


def shrink_rows(scalars, pieces, shrink_t, operand, spare):
    rank, depth = shrink_t.shape
    count = len(pieces)
    return pl.pallas_call(
        functools.partial(shrink_kernel, count),
        out_shape=jax.ShapeDtypeStruct(operand.shape, operand.dtype),
        in_specs=[pl.BlockSpec(memory_space=pltpu.SMEM)]
        + [ANY] * count
        + [pl.BlockSpec(memory_space=pltpu.VMEM), ANY],
        out_specs=ANY,
        scratch_shapes=[
            pltpu.VMEM((MOST * BLOCK, depth), jnp.bfloat16),
            pltpu.VMEM((spare,) + operand.shape[2:], jnp.bfloat16),
            pltpu.SemaphoreType.DMA((MOST,)),
            pltpu.SemaphoreType.DMA((operand.shape[0],)),
        ],
        input_output_aliases={2 + count: 0},
        compiler_params=pltpu.CompilerParams(vmem_limit_bytes=VMEM_LIMIT),
        cost_estimate=pl.CostEstimate(
            flops=2 * MOST * BLOCK * depth * rank, bytes_accessed=2 * MOST * BLOCK * depth, transcendentals=0
        ),
        name="shrink",
    )(scalars, *pieces, shrink_t, operand)


def base_kernel(count, scalars, *refs):
    pieces = refs[:count]
    weight, (out, rows, sem) = refs[count], refs[-3:]
    shard = pieces[0].shape[0]
    total = count * shard

    def copy(i):
        return pltpu.make_async_copy(pieces[i], rows.at[pl.ds(i * shard, shard)], sem.at[i])

    def product(first, last):
        found = jnp.dot(
            rows[first * shard : last * shard], weight[...], preferred_element_type=jnp.float32
        )
        for i in range(first, last):
            out[pl.ds(pl.multiple_of(scalars[i], shard), shard), :] = found[(i - first) * shard : (i - first + 1) * shard]

    @pl.when(pl.program_id(0) == 0)
    def _():
        for i in range(count):
            copy(i).start()
        for part in range(2):
            some = range(part * count // 2, (part + 1) * count // 2)
            for i in some:
                copy(i).wait()
            product(some[0], some[-1] + 1)

    @pl.when(pl.program_id(0) > 0)
    def _():
        product(0, count)


def base_matmul(places, pieces, weight, held, first, steps, tile):
    depth, columns = weight.shape
    count = len(pieces)
    rows = count * pieces[0].shape[0]
    extra = [] if held is None else [held]
    return pl.pallas_call(
        functools.partial(base_kernel, count),
        out_shape=jax.ShapeDtypeStruct((rows, columns), jnp.float32),
        grid_spec=pltpu.PrefetchScalarGridSpec(
            num_scalar_prefetch=1,
            grid=(steps,),
            in_specs=[ANY] * count + [pl.BlockSpec((depth, tile), lambda n, s: (0, first + n))] + [ANY] * len(extra),
            out_specs=pl.BlockSpec((rows, tile), lambda n, s: (0, first + n)),
            scratch_shapes=[pltpu.VMEM((rows, depth), jnp.bfloat16), pltpu.SemaphoreType.DMA((count,))],
        ),
        compiler_params=pltpu.CompilerParams(vmem_limit_bytes=VMEM_LIMIT),
        cost_estimate=pl.CostEstimate(
            flops=2 * rows * depth * tile * steps,
            bytes_accessed=2 * depth * tile * steps + 2 * rows * depth + 4 * rows * tile * steps,
            transcendentals=0,
        ),
        input_output_aliases={} if held is None else {count + 2: 0},
        name="base",
    )(places, *pieces, weight, *extra)


def last_kernel(spare, begins, base, shrunk, low, high, out, spread):
    width, tiles, height = low.shape[0], low.shape[1], low.shape[2]
    inner, others = width * height, high.shape[2]

    @pl.when(pl.program_id(0) == 0)
    def _():
        spread[...] = jnp.zeros_like(spread)
        half = LANES // 2
        for s in range(width):
            both = jnp.concatenate([shrunk[s, i] for i in range(spare)], axis=0)[:half]
            for h in range(2):
                rows = pl.ds(pl.multiple_of(begins[s] + h * half, BLOCK), half)
                mine = both[:, h * half : (h + 1) * half]
                spread[rows, s * height : (s + 1) * height] = mine[:, :height]
                spread[rows, inner + s * others : inner + (s + 1) * others] = mine[:, height:]

    expand = jnp.concatenate(
        [
            jnp.concatenate([part[:, t].reshape(width * part.shape[2], LANES) for t in range(tiles)], axis=1)
            for part in (low, high)
        ],
        axis=0,
    )
    lora = jnp.dot(spread[...], expand, preferred_element_type=jnp.float32).astype(jnp.bfloat16)
    out[...] = (base[...] + lora.astype(jnp.float32)).astype(jnp.bfloat16)


def last(begins, base, low, high, spare):
    total_rows, columns = base.shape
    width, all_tiles, height, _ = low.shape
    others = high.shape[2]
    tiles = 2 if all_tiles % 2 == 0 and spare % 2 == 0 else 1
    tile = tiles * LANES
    return pl.pallas_call(
        functools.partial(last_kernel, spare),
        out_shape=jax.ShapeDtypeStruct((total_rows, columns), jnp.bfloat16),
        grid_spec=pltpu.PrefetchScalarGridSpec(
            num_scalar_prefetch=1,
            grid=(columns // tile,),
            in_specs=[
                pl.BlockSpec((total_rows, tile), lambda n, s: (0, n)),
                pl.BlockSpec((width, spare, others, LANES), lambda n, s: (0, 0, 0, 0)),
                pl.BlockSpec((width, tiles, height, LANES), lambda n, s: (0, n, 0, 0)),
                pl.BlockSpec((width, tiles, others, LANES), lambda n, s: (0, n + spare // tiles, 0, 0)),
            ],
            out_specs=pl.BlockSpec((total_rows, tile), lambda n, s: (0, n)),
            scratch_shapes=[pltpu.VMEM((total_rows, width * (height + others)), jnp.bfloat16)],
        ),
        compiler_params=pltpu.CompilerParams(vmem_limit_bytes=VMEM_LIMIT),
        cost_estimate=pl.CostEstimate(
            flops=2 * total_rows * width * (height + others) * columns,
            bytes_accessed=6 * total_rows * columns + 2 * width * (height + others) * columns,
            transcendentals=0,
        ),
        name="last",
    )(begins, base, high, low, high)


def local(tokens, gate_weight, adapter_shrink, adapter_expand, adapter_blocks, adapter_position):
    width = lax.axis_size(AXIS)
    me = lax.axis_index(AXIS)
    shard, depth = tokens.shape
    columns = gate_weight.shape[1]
    rank = adapter_shrink.shape[2]
    total_rows = shard * width
    chips = width // 2
    chip_rows = 2 * shard
    chip, core = me // 2, me % 2

    count = adapter_position.shape[0]
    ids = jnp.arange(count, dtype=jnp.int32)
    capacity = MOST * BLOCK
    starts = jnp.sum(jnp.where(ids[None, :] < ids[:, None], adapter_blocks[None, :], 0), axis=1) * BLOCK
    sizes = adapter_blocks * BLOCK
    at_slot = adapter_position[None, :] == ids[:, None]
    start_by_slot = jnp.sum(jnp.where(at_slot, starts[None, :], 0), axis=1)
    size_by_slot = jnp.sum(jnp.where(at_slot, sizes[None, :], 0), axis=1)
    begin_by_slot = jnp.minimum(start_by_slot, total_rows - capacity)

    ring = list(range(0, chips, 2)) + list(range(chips - 1, 0, -2))
    place = [ring.index(a) for a in range(chips)]
    swap_core = [(a * 2 + c, a * 2 + 1 - c) for a in range(chips) for c in range(2)]
    around = [
        (a * 2 + c, ring[(place[a] + 1 - 2 * c) % chips] * 2 + c) for a in range(chips) for c in range(2)
    ]
    behind = jnp.asarray([[ring[(place[a] - j) % chips] for j in range(chips)] for a in range(chips)], jnp.int32)
    behind = lax.dynamic_index_in_dim(behind, chip, 0, keepdims=False)

    def send(value, pairs):
        return lax.ppermute(value, AXIS, pairs)

    shrink_t = jnp.swapaxes(adapter_shrink[0], 0, 1)
    height = rank // 2
    spare = -(-(MOST * BLOCK // 2) // (rank - height))

    low, high = parts_of(adapter_expand[0], height, width, spare)
    half_way = chips // 2
    first = send(tokens, around)
    neighbour = send(tokens, swap_core)
    second = send(neighbour, around)
    pieces = [tokens, neighbour]
    places = [me * shard, (chip * 2 + 1 - core) * shard]
    swapped = [neighbour]
    for j in range(1, half_way + 1):
        mine_from = jnp.where(core == 0, behind[j], behind[chips - j]) * 2
        other_from = jnp.where(core == 0, behind[chips - j], behind[j]) * 2
        if j < half_way:
            first, second = order([first, second], swapped + [low, high])
            next_first = send(first, around)
            next_second = send(second, around) if j + 1 < half_way else None
            swapped = [send(first, swap_core), send(second, swap_core)]
            pieces += [first, second] + swapped
            places += [
                (mine_from + core) * shard,
                (mine_from + 1 - core) * shard,
                (other_from + 1 - core) * shard,
                (other_from + core) * shard,
            ]
            first, second = next_first, next_second
        else:
            low = order([low], [first] + swapped)[0]
            swapped.append(send(first, swap_core))
            low = lax.all_to_all(low, AXIS, split_axis=0, concat_axis=0, tiled=True)
            pieces += [first, swapped[-1]]
            places += [(mine_from + core) * shard, (other_from + 1 - core) * shard]
    places = jnp.stack(places).astype(jnp.int32)

    mine = jnp.stack([begin_by_slot[me], start_by_slot[me], size_by_slot[me]])
    scalars = jnp.concatenate([places, mine]).astype(jnp.int32)
    high = shrink_rows(scalars, pieces, shrink_t, high, spare)
    tile = 256
    while columns % tile or total_rows * tile > 1024 * 256:
        tile //= 2
    steps = columns // tile
    early = max(steps // 7, 1)
    places = order([places], [high])[0]
    base = base_matmul(places, pieces, gate_weight, None, 0, early, tile)
    high, base, places = order([high, base, places], [low])
    high = lax.all_to_all(high, AXIS, split_axis=0, concat_axis=0, tiled=True)
    base = base_matmul(places, pieces, gate_weight, base, early, steps - early, tile)
    return last(begin_by_slot.astype(jnp.int32), base, low, high, spare)


def solution(mesh):
    return jax.shard_map(
        local,
        mesh=mesh,
        in_specs=(
            P(("groups", "tensor"), None),
            P(None, "tensor"),
            P(("groups", "tensor"), None, None),
            P(("groups", "tensor"), None, None),
            P("groups"),
            P("groups"),
        ),
        out_specs=P("groups", "tensor"),
        check_vma=False,
    )
```

time: 394 us -> 209 us (0.53)
  waiting for transfers between devices: 282 us -> 88.1 us
  Pallas kernels: 0 us -> 75.9 us
  matrix products: 52.9 us -> 0 us
  other arithmetic: 30.9 us -> 0.24 us
  starting transfers between devices: 7.74 us -> 25.4 us
  between operations: 15.4 us -> 8.17 us
  local copies, waits for them, and re-layouts: 4.77 us -> 10.9 us
    all_to_all x1 -> x2, waiting for transfers between devices: 160 us -> 13.1 us  [the longest x1 7.99 us: local(): high = lax.all_to_all(high, AXIS, split_axis=0, concat_axis=0, tiled=True)]
    all_gather x1 -> x0, waiting for transfers between devices: 122 us -> none  [local(): piece = lax.all_gather(tokens, 'tensor', axis=0, tiled=True)]
    pallas_call x0 -> x5, Pallas kernels: none -> 75.9 us  [the longest x2 55.8 us: base_matmul(): pl.pallas_call(functools.partial(base_kernel, count), out_shape=jax.Shape...]
    ppermute x0 -> x15, waiting for transfers between devices: none -> 75 us  [send(): return lax.ppermute(value, AXIS, pairs)]
    dot_general x3 -> x0, matrix products: 52.9 us -> none  [the longest x1 39.6 us: local(): base_part = jnp.dot(piece, gate_weight, preferred_element_type=jnp.float32)]
    scatter-add x1 -> x0, other arithmetic: 27.8 us -> none  [local(): adapter_output = jnp.zeros((gathered_rows, column_width), jnp.bfloat16).a...]
    ppermute x0 -> x15, starting transfers between devices: none -> 13.7 us  [send(): return lax.ppermute(value, AXIS, pairs)]
    unnamed x6 -> x38, local copies, waits for them, and re-layouts: 0.01 us -> 4.66 us
  transfers between devices with their start and end apart: 2 -> 17, of which waited for: 2 -> 11; matrix products, arithmetic and copies ran while one was open for 1% -> 3% of each run, Pallas kernels for 0% -> 31%
where the time goes in v3:
time: 209 us
  waiting for transfers between devices  88.1 us (42%)
  Pallas kernels  75.9 us (36%)
  starting transfers between devices  25.4 us (12%)
  local copies, waits for them, and re-layouts  10.9 us (5%)
  between operations  8.17 us (4%)
    ppermute x15, waiting for transfers between devices, send(): return lax.ppermute(value, AXIS, pairs)  75 us
    pallas_call x2, Pallas kernels, base_matmul(): pl.pallas_call(functools.partial(base_kernel, count), out_shape=jax.Shape...  55.8 us
    ppermute x15, starting transfers between devices, send(): return lax.ppermute(value, AXIS, pairs)  13.7 us
    pallas_call x1, Pallas kernels, last(): pl.pallas_call(functools.partial(last_kernel, spare), out_shape=jax.Shape...  11.1 us
    all_to_all x1, waiting for transfers between devices, local(): high = lax.all_to_all(high, AXIS, split_axis=0, concat_axis=0, tiled=True)  7.99 us
    all_to_all x1, starting transfers between devices, local(): low = lax.all_to_all(low, AXIS, split_axis=0, concat_axis=0, tiled=True)  6.81 us
    all_to_all x1, waiting for transfers between devices, local(): low = lax.all_to_all(low, AXIS, split_axis=0, concat_axis=0, tiled=True)  5.07 us
    all_to_all x1, starting transfers between devices, local(): high = lax.all_to_all(high, AXIS, split_axis=0, concat_axis=0, tiled=True)  4.91 us
  transfers between devices with their start and end apart: 17, of which 11 were waited for; matrix products, arithmetic and copies ran while one was open for 3% of the time, Pallas kernels for 31%

profile of v3, /device:TPU:13, one launch (start us, length us, event | category | flops | bytes accessed | tf_op | source)
XLA Modules:
  0.0 208.7 jit_solution(128216402498572312)
XLA Ops:
  0.7 1.3 collective-permute-start.1
  2.0 1.2 collective-permute-done.refs_1_
  3.2 1.3 collective-permute-start.2
  4.5 4.7 %parts.1 = (bf16[16,14,32,128]{3,2,1,0:T(8,128)(2,1)}, bf16[16,16,32,128]{3,2,1,0:T(8,128)(2,1)}) custom-call(bf16[64,28672]{1,0:T(8,128)(2,1)} %bitcast.27), custom_call_target="tpu_custom_call" | custom-call | bytes 7340032 | tf_op jit(solution)/shard_map/parts/pallas_call | solution.py:35
  9.2 5.7 %collective-permute-done.1.refs_2_ = bf16[64,8192]{1,0:T(8,128)(2,1)S(1)} collective-permute-done((bf16[64,8192]{1,0:T(8,128)(2,1)}, bf16[64,8192]{1,0:T(8,128)(2,1)S(1)}, u32[]{:S(2)}, u32[]{:S(2)}) %collective-permute-start.1) | collective-permute-done | bytes 1048608 | tf_op jit(solution)/shard_map/ppermute | solution.py:267
  14.8 11.2 %collective-permute-done.2.refs_3_ = bf16[64,8192]{1,0:T(8,128)(2,1)S(1)} collective-permute-done((bf16[64,8192]{1,0:T(8,128)(2,1)S(1)}, bf16[64,8192]{1,0:T(8,128)(2,1)S(1)}, u32[]{:S(2)}, u32[]{:S(2)}) %collective-permute-start.2) | collective-permute-done | bytes 1048608 | tf_op jit(solution)/shard_map/ppermute | solution.py:267
  26.1 1.3 collective-permute-start.5
  27.4 1.3 collective-permute-start.6
  28.7 11.3 %collective-permute-done.5.refs_6_ = bf16[64,8192]{1,0:T(8,128)(2,1)S(1)} collective-permute-done((bf16[64,8192]{1,0:T(8,128)(2,1)S(1)}, bf16[64,8192]{1,0:T(8,128)(2,1)S(1)}, u32[]{:S(2)}, u32[]{:S(2)}) %collective-permute-start.5) | collective-permute-done | bytes 1048608 | tf_op jit(solution)/shard_map/ppermute | solution.py:267
  40.0 11.2 %collective-permute-done.6.refs_7_ = bf16[64,8192]{1,0:T(8,128)(2,1)S(1)} collective-permute-done((bf16[64,8192]{1,0:T(8,128)(2,1)S(1)}, bf16[64,8192]{1,0:T(8,128)(2,1)S(1)}, u32[]{:S(2)}, u32[]{:S(2)}) %collective-permute-start.6) | collective-permute-done | bytes 1048608 | tf_op jit(solution)/shard_map/ppermute | solution.py:267
  51.3 1.3 collective-permute-start.9
  52.6 0.9 collective-permute-start.7
  53.5 1.3 collective-permute-start.10
  54.8 10.5 %collective-permute-done.9.refs_10_ = bf16[64,8192]{1,0:T(8,128)(2,1)S(1)} collective-permute-done((bf16[64,8192]{1,0:T(8,128)(2,1)S(1)}, bf16[64,8192]{1,0:T(8,128)(2,1)S(1)}, u32[]{:S(2)}, u32[]{:S(2)}) %collective-permute-start.9) | collective-permute-done | bytes 1048608 | tf_op jit(solution)/shard_map/ppermute | solution.py:267
  65.3 11.2 %collective-permute-done.10.refs_11_ = bf16[64,8192]{1,0:T(8,128)(2,1)S(1)} collective-permute-done((bf16[64,8192]{1,0:T(8,128)(2,1)S(1)}, bf16[64,8192]{1,0:T(8,128)(2,1)S(1)}, u32[]{:S(2)}, u32[]{:S(2)}) %collective-permute-start.10) | collective-permute-done | bytes 1048608 | tf_op jit(solution)/shard_map/ppermute | solution.py:267
  76.5 2.6 %collective-permute-start.12 = (bf16[64,8192]{1,0:T(8,128)(2,1)S(1)}, bf16[64,8192]{1,0:T(8,128)(2,1)S(1)}, u32[]{:S(2)}, u32[]{:S(2)}) collective-permute-start(bf16[64,8192]{1,0:T(8,128)(2,1)S(1)} %collective-permute-done.10.refs_11_), channel_id=1, source_target_pairs={{0,1},{1,0},{2,3},{3,2},{4,5},{5,4},{6,7},{7,6},{8,9},{9,8},{10,11... | collective-permute-start | bytes 3145736 | tf_op jit(solution)/shard_map/ppermute | solution.py:267
  79.1 1.3 collective-permute-start.13
  80.4 1.0 collective-permute-done.12.refs_13_
  81.4 11.7 %collective-permute-done.13.refs_14_ = bf16[64,8192]{1,0:T(8,128)(2,1)S(1)} collective-permute-done((bf16[64,8192]{1,0:T(8,128)(2,1)S(1)}, bf16[64,8192]{1,0:T(8,128)(2,1)S(1)}, u32[]{:S(2)}, u32[]{:S(2)}) %collective-permute-start.13) | collective-permute-done | bytes 1048608 | tf_op jit(solution)/shard_map/ppermute | solution.py:267
  93.1 1.0 copy-done.14
  94.1 6.8 %all-to-all-start = ((bf16[16,14,32,128]{3,2,1,0:T(8,128)(2,1)}), bf16[16,14,32,128]{3,2,1,0:T(8,128)(2,1)S(1)}, u32[]{:S(2)}, u32[]{:S(2)}) async-start(bf16[16,14,32,128]{3,2,1,0:T(8,128)(2,1)} %get-tuple-element.27), calls=%async_computation | async-start | bytes 3670016 | tf_op jit(solution)/shard_map/all_to_all | solution.py:300
  113.3 2.5 %concatenate.4.scalars = s32[19]{0:T(128)} concatenate(s32[1]{0:T(128)} %bitcast, s32[1]{0:T(128)} %bitcast.1, s32[1]{0:T(128)} %bitcast.4, s32[1]{0:T(128)} %bitcast.5, s32[1]{0:T(128)} %bitcast.6, s32[1]{0:T(128)} %bitcast.7, s32[1]{0:T(128)} %bitcast.10, s32[1]{0:T(128)} %bitcast.11, s32[1]{0:T(128)} %bitcast.12, s32[1]{0:T(128)} %bitcast.13, s32[1]{0:T(128)} %bitcast.16, ...), dimensions={0} | concatenate | bytes 152 | tf_op jit(solution)/shard_map/concatenate | solution.py:306
  115.8 1.0 copy-done.15
  116.9 4.4 %shrink.1 = bf16[16,16,32,128]{3,2,1,0:T(8,128)(2,1)} custom-call(s32[19]{0:T(128)} %concatenate.4.scalars, bf16[64,8192]{1,0:T(8,128)(2,1)} %refs_0_.5, bf16[64,8192]{1,0:T(8,128)(2,1)} %copy-done.2, bf16[64,8192]{1,0:T(8,128)(2,1)} %copy-done.3, bf16[64,8192]{1,0:T(8,128)(2,1)} %copy-done.4, ...), custom_call_target="tpu_custom_call", output_to_operand_aliasing={{}: (18, {})} | custom-call | flops 134217728 | bytes 2097152 | tf_op jit(solution)/shard_map/shrink/pallas_call | solution.py:99
  121.3 16.3 %base.2.refs_17_ = f32[1024,1792]{1,0:T(8,128)} custom-call(s32[16]{0:T(128)} %stack.67.scalars, bf16[64,8192]{1,0:T(8,128)(2,1)} %refs_0_.5, bf16[64,8192]{1,0:T(8,128)(2,1)} %copy-done.2, bf16[64,8192]{1,0:T(8,128)(2,1)} %copy-done.3, bf16[64,8192]{1,0:T(8,128)(2,1)} %copy-done.4, bf16[64,8192]{1,0:T(8,128)(2,1)} %copy-done.6, bf16[64,8192]{1,0:T(8,128)(2,1)} %copy-done.8, ...), custom_call_target="tpu_custom_call" | custom-call | flops 4294967296 | bytes 22020096 | tf_op jit(solution)/shard_map/base/pallas_call | solution.py:157
  137.6 5.1 %all-to-all-done.low = bf16[16,14,32,128]{3,2,1,0:T(8,128)(2,1)S(1)} async-done(((bf16[16,14,32,128]{3,2,1,0:T(8,128)(2,1)}), bf16[16,14,32,128]{3,2,1,0:T(8,128)(2,1)S(1)}, u32[]{:S(2)}, u32[]{:S(2)}) %all-to-all-start) | async-done | bytes 1835040 | tf_op jit(solution)/shard_map/all_to_all | solution.py:300
  142.7 1.2 copy-done.1
  143.9 4.9 %all-to-all-start.1 = ((bf16[16,16,32,128]{3,2,1,0:T(8,128)(2,1)}), bf16[16,16,32,128]{3,2,1,0:T(8,128)(2,1)S(1)}, u32[]{:S(2)}, u32[]{:S(2)}) async-start(bf16[16,16,32,128]{3,2,1,0:T(8,128)(2,1)} %shrink.1), calls=%async_computation.1 | async-start | bytes 4194304 | tf_op jit(solution)/shard_map/all_to_all | solution.py:316
  148.9 39.4 %base.3 = f32[1024,1792]{1,0:T(8,128)} custom-call(s32[16]{0:T(128)} %stack.67.scalars, bf16[64,8192]{1,0:T(8,128)(2,1)} %refs_0_.5, bf16[64,8192]{1,0:T(8,128)(2,1)} %copy-done.2, bf16[64,8192]{1,0:T(8,128)(2,1)} %copy-done.3, bf16[64,8192]{1,0:T(8,128)(2,1)} %copy-done.4, bf16[64,8192]{1,0:T(8,128)(2,1)} %copy-done.6, ...), custom_call_target="tpu_custom_call", output_to_operand_aliasing={{}: (18, {})} | custom-call | flops 25769803776 | bytes 48234496 | tf_op jit(solution)/shard_map/base/pallas_call | solution.py:157
  188.3 8.0 %all-to-all-done.1.shrunk.high = bf16[16,16,32,128]{3,2,1,0:T(8,128)(2,1)S(1)} async-done(((bf16[16,16,32,128]{3,2,1,0:T(8,128)(2,1)}), bf16[16,16,32,128]{3,2,1,0:T(8,128)(2,1)S(1)}, u32[]{:S(2)}, u32[]{:S(2)}) %all-to-all-start.1) | async-done | bytes 2097184 | tf_op jit(solution)/shard_map/all_to_all | solution.py:316
  196.3 1.4 copy-done
  197.6 11.1 %last.1 = bf16[1024,1792]{1,0:T(8,128)(2,1)} custom-call(s32[16]{0:T(128)} %copy-done.16, f32[1024,1792]{1,0:T(8,128)} %base.3, bf16[16,16,32,128]{3,2,1,0:T(8,128)(2,1)} %copy-done, bf16[16,14,32,128]{3,2,1,0:T(8,128)(2,1)} %copy-done.1, bf16[16,16,32,128]{3,2,1,0:T(8,128)(2,1)} %copy-done), custom_call_target="tpu_custom_call" | custom-call | flops 3758096384 | bytes 14680064 | tf_op jit(solution)/shard_map/last/pallas_call | solution.py:211
  (56 shorter events, 5.1 us)
Async XLA Ops:
  0.0 3.2 %collective-permute-start = (bf16[64,8192]{1,0:T(8,128)(2,1)}, bf16[64,8192]{1,0:T(8,128)(2,1)S(1)}, u32[]{:S(2)}, u32[]{:S(2)}) collective-permute-start(bf16[64,8192]{1,0:T(8,128)(2,1)} %refs_0_.5), channel_id=1, source_target_pairs={{0,1},{1,0},{2,3},{3,2},{4,5},{5,4},{6,7},{7,6},{8,9},{9,8},{10,11... | collective-permute-start | bytes 3145736 | tf_op jit(solution)/shard_map/ppermute | solution.py:267
  0.7 14.2 %collective-permute-start.1 = (bf16[64,8192]{1,0:T(8,128)(2,1)}, bf16[64,8192]{1,0:T(8,128)(2,1)S(1)}, u32[]{:S(2)}, u32[]{:S(2)}) collective-permute-start(bf16[64,8192]{1,0:T(8,128)(2,1)} %refs_0_.5), channel_id=1, source_target_pairs={{0,4},{1,3},{2,0},{3,7},{4,8},{5,1},{6,2},{7,11},{8,12},{9,5},{10,... | collective-permute-start | bytes 3145736 | tf_op jit(solution)/shard_map/ppermute | solution.py:267
  3.2 90.9 %copy-start.2 = (bf16[64,8192]{1,0:T(8,128)(2,1)}, bf16[64,8192]{1,0:T(8,128)(2,1)S(1)}, u32[]{:S(2)}) copy-start(bf16[64,8192]{1,0:T(8,128)(2,1)S(1)} %collective-permute-done.refs_1_) | copy-start | bytes 3145732
  3.2 22.9 %collective-permute-start.2 = (bf16[64,8192]{1,0:T(8,128)(2,1)S(1)}, bf16[64,8192]{1,0:T(8,128)(2,1)S(1)}, u32[]{:S(2)}, u32[]{:S(2)}) collective-permute-start(bf16[64,8192]{1,0:T(8,128)(2,1)S(1)} %collective-permute-done.refs_1_), channel_id=1, source_target_pairs={{0,4},{1,3},{2,0},{3,7},{4,8},{5,1},{6,2},{7,11},{8,12},{9,5},{10,... | collective-permute-start | bytes 3145736 | tf_op jit(solution)/shard_map/ppermute | solution.py:267
  4.5 106.2 %copy-start.18 = (s32[16]{0:T(128)S(1)}, s32[16]{0:T(128)}, u32[]{:S(2)}) copy-start(s32[16]{0:T(128)} %param.11) | copy-start | bytes 196
  4.5 106.3 %copy-start.17 = (s32[16]{0:T(128)S(1)}, s32[16]{0:T(128)}, u32[]{:S(2)}) copy-start(s32[16]{0:T(128)} %param.12) | copy-start | bytes 196
  14.8 12.5 %copy-start.3 = (bf16[64,8192]{1,0:T(8,128)(2,1)}, bf16[64,8192]{1,0:T(8,128)(2,1)S(1)}, u32[]{:S(2)}) copy-start(bf16[64,8192]{1,0:T(8,128)(2,1)S(1)} %collective-permute-done.1.refs_2_) | copy-start | bytes 3145732
  26.1 14.0 %copy-start.4 = (bf16[64,8192]{1,0:T(8,128)(2,1)}, bf16[64,8192]{1,0:T(8,128)(2,1)S(1)}, u32[]{:S(2)}) copy-start(bf16[64,8192]{1,0:T(8,128)(2,1)S(1)} %collective-permute-done.2.refs_3_) | copy-start | bytes 3145732
  26.1 13.9 %collective-permute-start.5 = (bf16[64,8192]{1,0:T(8,128)(2,1)S(1)}, bf16[64,8192]{1,0:T(8,128)(2,1)S(1)}, u32[]{:S(2)}, u32[]{:S(2)}) collective-permute-start(bf16[64,8192]{1,0:T(8,128)(2,1)S(1)} %collective-permute-done.1.refs_2_), channel_id=1, source_target_pairs={{0,4},{1,3},{2,0},{3,7},{4,8},{5,1},{6,2},{7,11},{8,12},{9,5},{10,... | collective-permute-start | bytes 3145736 | tf_op jit(solution)/shard_map/ppermute | solution.py:267
  27.4 12.7 %collective-permute-start.3 = (bf16[64,8192]{1,0:T(8,128)(2,1)S(1)}, bf16[64,8192]{1,0:T(8,128)(2,1)S(1)}, u32[]{:S(2)}, u32[]{:S(2)}) collective-permute-start(bf16[64,8192]{1,0:T(8,128)(2,1)S(1)} %collective-permute-done.1.refs_2_), channel_id=1, source_target_pairs={{0,1},{1,0},{2,3},{3,2},{4,5},{5,4},{6,7},{7,6},{8,9},{9,8},{10,11... | collective-permute-start | bytes 3145736 | tf_op jit(solution)/shard_map/ppermute | solution.py:267
  27.4 23.9 %collective-permute-start.6 = (bf16[64,8192]{1,0:T(8,128)(2,1)S(1)}, bf16[64,8192]{1,0:T(8,128)(2,1)S(1)}, u32[]{:S(2)}, u32[]{:S(2)}) collective-permute-start(bf16[64,8192]{1,0:T(8,128)(2,1)S(1)} %collective-permute-done.2.refs_3_), channel_id=1, source_target_pairs={{0,4},{1,3},{2,0},{3,7},{4,8},{5,1},{6,2},{7,11},{8,12},{9,5},{10,... | collective-permute-start | bytes 3145736 | tf_op jit(solution)/shard_map/ppermute | solution.py:267
  28.7 22.6 %collective-permute-start.4 = (bf16[64,8192]{1,0:T(8,128)(2,1)S(1)}, bf16[64,8192]{1,0:T(8,128)(2,1)S(1)}, u32[]{:S(2)}, u32[]{:S(2)}) collective-permute-start(bf16[64,8192]{1,0:T(8,128)(2,1)S(1)} %collective-permute-done.2.refs_3_), channel_id=1, source_target_pairs={{0,1},{1,0},{2,3},{3,2},{4,5},{5,4},{6,7},{7,6},{8,9},{9,8},{10,11... | collective-permute-start | bytes 3145736 | tf_op jit(solution)/shard_map/ppermute | solution.py:267
  40.0 12.6 %copy-start.5 = (bf16[64,8192]{1,0:T(8,128)(2,1)}, bf16[64,8192]{1,0:T(8,128)(2,1)S(1)}, u32[]{:S(2)}) copy-start(bf16[64,8192]{1,0:T(8,128)(2,1)S(1)} %collective-permute-done.5.refs_6_) | copy-start | bytes 3145732
  40.0 25.2 %copy-start.6 = (bf16[64,8192]{1,0:T(8,128)(2,1)}, bf16[64,8192]{1,0:T(8,128)(2,1)S(1)}, u32[]{:S(2)}) copy-start(bf16[64,8192]{1,0:T(8,128)(2,1)S(1)} %collective-permute-done.3.refs_4_) | copy-start | bytes 3145732
  51.2 25.2 %copy-start.7 = (bf16[64,8192]{1,0:T(8,128)(2,1)}, bf16[64,8192]{1,0:T(8,128)(2,1)S(1)}, u32[]{:S(2)}) copy-start(bf16[64,8192]{1,0:T(8,128)(2,1)S(1)} %collective-permute-done.6.refs_7_) | copy-start | bytes 3145732
  51.3 42.8 %copy-start.8 = (bf16[64,8192]{1,0:T(8,128)(2,1)}, bf16[64,8192]{1,0:T(8,128)(2,1)S(1)}, u32[]{:S(2)}) copy-start(bf16[64,8192]{1,0:T(8,128)(2,1)S(1)} %collective-permute-done.4.refs_5_) | copy-start | bytes 3145732
  51.3 14.0 %collective-permute-start.9 = (bf16[64,8192]{1,0:T(8,128)(2,1)S(1)}, bf16[64,8192]{1,0:T(8,128)(2,1)S(1)}, u32[]{:S(2)}, u32[]{:S(2)}) collective-permute-start(bf16[64,8192]{1,0:T(8,128)(2,1)S(1)} %collective-permute-done.5.refs_6_), channel_id=1, source_target_pairs={{0,4},{1,3},{2,0},{3,7},{4,8},{5,1},{6,2},{7,11},{8,12},{9,5},{10,... | collective-permute-start | bytes 3145736 | tf_op jit(solution)/shard_map/ppermute | solution.py:267
  52.6 12.6 %collective-permute-start.7 = (bf16[64,8192]{1,0:T(8,128)(2,1)S(1)}, bf16[64,8192]{1,0:T(8,128)(2,1)S(1)}, u32[]{:S(2)}, u32[]{:S(2)}) collective-permute-start(bf16[64,8192]{1,0:T(8,128)(2,1)S(1)} %collective-permute-done.5.refs_6_), channel_id=1, source_target_pairs={{0,1},{1,0},{2,3},{3,2},{4,5},{5,4},{6,7},{7,6},{8,9},{9,8},{10,11... | collective-permute-start | bytes 3145736 | tf_op jit(solution)/shard_map/ppermute | solution.py:267
  53.5 23.0 %collective-permute-start.10 = (bf16[64,8192]{1,0:T(8,128)(2,1)S(1)}, bf16[64,8192]{1,0:T(8,128)(2,1)S(1)}, u32[]{:S(2)}, u32[]{:S(2)}) collective-permute-start(bf16[64,8192]{1,0:T(8,128)(2,1)S(1)} %collective-permute-done.6.refs_7_), channel_id=1, source_target_pairs={{0,4},{1,3},{2,0},{3,7},{4,8},{5,1},{6,2},{7,11},{8,12},{9,5},{10,... | collective-permute-start | bytes 3145736 | tf_op jit(solution)/shard_map/ppermute | solution.py:267
  54.8 21.7 %collective-permute-start.8 = (bf16[64,8192]{1,0:T(8,128)(2,1)S(1)}, bf16[64,8192]{1,0:T(8,128)(2,1)S(1)}, u32[]{:S(2)}, u32[]{:S(2)}) collective-permute-start(bf16[64,8192]{1,0:T(8,128)(2,1)S(1)} %collective-permute-done.6.refs_7_), channel_id=1, source_target_pairs={{0,1},{1,0},{2,3},{3,2},{4,5},{5,4},{6,7},{7,6},{8,9},{9,8},{10,11... | collective-permute-start | bytes 3145736 | tf_op jit(solution)/shard_map/ppermute | solution.py:267
  65.2 15.2 %copy-start.9 = (bf16[64,8192]{1,0:T(8,128)(2,1)}, bf16[64,8192]{1,0:T(8,128)(2,1)S(1)}, u32[]{:S(2)}) copy-start(bf16[64,8192]{1,0:T(8,128)(2,1)S(1)} %collective-permute-done.9.refs_10_) | copy-start | bytes 3145732
  65.3 27.8 %copy-start.10 = (bf16[64,8192]{1,0:T(8,128)(2,1)}, bf16[64,8192]{1,0:T(8,128)(2,1)S(1)}, u32[]{:S(2)}) copy-start(bf16[64,8192]{1,0:T(8,128)(2,1)S(1)} %collective-permute-done.7.refs_8_) | copy-start | bytes 3145732
  76.5 16.6 %copy-start.11 = (bf16[64,8192]{1,0:T(8,128)(2,1)}, bf16[64,8192]{1,0:T(8,128)(2,1)S(1)}, u32[]{:S(2)}) copy-start(bf16[64,8192]{1,0:T(8,128)(2,1)S(1)} %collective-permute-done.10.refs_11_) | copy-start | bytes 3145732
  76.5 16.6 %copy-start.12 = (bf16[64,8192]{1,0:T(8,128)(2,1)}, bf16[64,8192]{1,0:T(8,128)(2,1)S(1)}, u32[]{:S(2)}) copy-start(bf16[64,8192]{1,0:T(8,128)(2,1)S(1)} %collective-permute-done.8.refs_9_) | copy-start | bytes 3145732
  76.5 4.9 %collective-permute-start.12 = (bf16[64,8192]{1,0:T(8,128)(2,1)S(1)}, bf16[64,8192]{1,0:T(8,128)(2,1)S(1)}, u32[]{:S(2)}, u32[]{:S(2)}) collective-permute-start(bf16[64,8192]{1,0:T(8,128)(2,1)S(1)} %collective-permute-done.10.refs_11_), channel_id=1, source_target_pairs={{0,1},{1,0},{2,3},{3,2},{4,5},{5,4},{6,7},{7,6},{8,9},{9,8},{10,11... | collective-permute-start | bytes 3145736 | tf_op jit(solution)/shard_map/ppermute | solution.py:267
  79.1 13.9 %collective-permute-start.13 = (bf16[64,8192]{1,0:T(8,128)(2,1)S(1)}, bf16[64,8192]{1,0:T(8,128)(2,1)S(1)}, u32[]{:S(2)}, u32[]{:S(2)}) collective-permute-start(bf16[64,8192]{1,0:T(8,128)(2,1)S(1)} %collective-permute-done.9.refs_10_), channel_id=1, source_target_pairs={{0,4},{1,3},{2,0},{3,7},{4,8},{5,1},{6,2},{7,11},{8,12},{9,5},{10,... | collective-permute-start | bytes 3145736 | tf_op jit(solution)/shard_map/ppermute | solution.py:267
  80.4 13.7 %collective-permute-start.11 = (bf16[64,8192]{1,0:T(8,128)(2,1)S(1)}, bf16[64,8192]{1,0:T(8,128)(2,1)}, u32[]{:S(2)}, u32[]{:S(2)}) collective-permute-start(bf16[64,8192]{1,0:T(8,128)(2,1)S(1)} %collective-permute-done.9.refs_10_), channel_id=1, source_target_pairs={{0,1},{1,0},{2,3},{3,2},{4,5},{5,4},{6,7},{7,6},{8,9},{9,8},{10,11... | collective-permute-start | bytes 3145736 | tf_op jit(solution)/shard_map/ppermute | solution.py:267
  81.4 11.7 %copy-start.13 = (bf16[64,8192]{1,0:T(8,128)(2,1)}, bf16[64,8192]{1,0:T(8,128)(2,1)S(1)}, u32[]{:S(2)}) copy-start(bf16[64,8192]{1,0:T(8,128)(2,1)S(1)} %collective-permute-done.12.refs_13_) | copy-start | bytes 3145732
  94.1 48.6 %all-to-all-start = ((bf16[16,14,32,128]{3,2,1,0:T(8,128)(2,1)}), bf16[16,14,32,128]{3,2,1,0:T(8,128)(2,1)S(1)}, u32[]{:S(2)}, u32[]{:S(2)}) async-start(bf16[16,14,32,128]{3,2,1,0:T(8,128)(2,1)} %get-tuple-element.27), calls=%async_computation | async-start | bytes 3670016 | tf_op jit(solution)/shard_map/all_to_all | solution.py:300
  100.9 14.9 %collective-permute-start.14 = (bf16[64,8192]{1,0:T(8,128)(2,1)}, bf16[64,8192]{1,0:T(8,128)(2,1)S(1)}, u32[]{:S(2)}, u32[]{:S(2)}) collective-permute-start(bf16[64,8192]{1,0:T(8,128)(2,1)} %copy-done.14), channel_id=1, source_target_pairs={{0,1},{1,0},{2,3},{3,2},{4,5},{5,4},{6,7},{7,6},{8,9},{9,8},{10,11... | collective-permute-start | bytes 3145736 | tf_op jit(solution)/shard_map/ppermute | solution.py:267
  112.2 9.1 %copy-start.16 = (s32[16]{0:T(128)}, s32[16]{0:T(128)S(1)}, u32[]{:S(2)}) copy-start(s32[16]{0:T(128)S(1)} %broadcast_minimum_fusion.begins) | copy-start | bytes 196
  143.9 52.3 %all-to-all-start.1 = ((bf16[16,16,32,128]{3,2,1,0:T(8,128)(2,1)}), bf16[16,16,32,128]{3,2,1,0:T(8,128)(2,1)S(1)}, u32[]{:S(2)}, u32[]{:S(2)}) async-start(bf16[16,16,32,128]{3,2,1,0:T(8,128)(2,1)} %shrink.1), calls=%async_computation.1 | async-start | bytes 4194304 | tf_op jit(solution)/shard_map/all_to_all | solution.py:316
  (4 other events, 4.6 us)

commit v4 on v3

--- a/solution.py
+++ b/solution.py
@@ -118,64 +118,50 @@
     )(scalars, *pieces, shrink_t, operand)
 
 
-def base_kernel(count, scalars, *refs):
+def base_kernel(count, *refs):
     pieces = refs[:count]
-    weight, (out, rows, sem) = refs[count], refs[-3:]
+    weight, out, rows, sem = refs[count:]
     shard = pieces[0].shape[0]
-    total = count * shard
-
-    def copy(i):
-        return pltpu.make_async_copy(pieces[i], rows.at[pl.ds(i * shard, shard)], sem.at[i])
-
-    def product(first, last):
-        found = jnp.dot(
-            rows[first * shard : last * shard], weight[...], preferred_element_type=jnp.float32
-        )
-        for i in range(first, last):
-            out[pl.ds(pl.multiple_of(scalars[i], shard), shard), :] = found[(i - first) * shard : (i - first + 1) * shard]
 
     @pl.when(pl.program_id(0) == 0)
     def _():
-        for i in range(count):
-            copy(i).start()
-        for part in range(2):
-            some = range(part * count // 2, (part + 1) * count // 2)
-            for i in some:
-                copy(i).wait()
-            product(some[0], some[-1] + 1)
-
-    @pl.when(pl.program_id(0) > 0)
-    def _():
-        product(0, count)
-
-
-def base_matmul(places, pieces, weight, held, first, steps, tile):
+        copies = [
+            pltpu.make_async_copy(pieces[i], rows.at[pl.ds(i * shard, shard)], sem.at[i]) for i in range(count)
+        ]
+        for copy in copies:
+            copy.start()
+        for copy in copies:
+            copy.wait()
+
+    out[...] = jnp.dot(rows[...], weight[...], preferred_element_type=jnp.float32)
+
+
+def base_matmul(pieces, weight, share=1, tile=256):
     depth, columns = weight.shape
     count = len(pieces)
     rows = count * pieces[0].shape[0]
-    extra = [] if held is None else [held]
+    while columns % tile:
+        tile //= 2
     return pl.pallas_call(
         functools.partial(base_kernel, count),
         out_shape=jax.ShapeDtypeStruct((rows, columns), jnp.float32),
-        grid_spec=pltpu.PrefetchScalarGridSpec(
-            num_scalar_prefetch=1,
-            grid=(steps,),
-            in_specs=[ANY] * count + [pl.BlockSpec((depth, tile), lambda n, s: (0, first + n))] + [ANY] * len(extra),
-            out_specs=pl.BlockSpec((rows, tile), lambda n, s: (0, first + n)),
-            scratch_shapes=[pltpu.VMEM((rows, depth), jnp.bfloat16), pltpu.SemaphoreType.DMA((count,))],
-        ),
+        grid=(columns // tile,),
+        in_specs=[ANY] * count + [pl.BlockSpec((depth, tile), lambda n: (0, n))],
+        out_specs=pl.BlockSpec((rows, tile), lambda n: (0, n)),
+        scratch_shapes=[pltpu.VMEM((rows, depth), jnp.bfloat16), pltpu.SemaphoreType.DMA((count,))],
         compiler_params=pltpu.CompilerParams(vmem_limit_bytes=VMEM_LIMIT),
         cost_estimate=pl.CostEstimate(
-            flops=2 * rows * depth * tile * steps,
-            bytes_accessed=2 * depth * tile * steps + 2 * rows * depth + 4 * rows * tile * steps,
+            flops=2 * rows * depth * columns * share,
+            bytes_accessed=2 * depth * columns + 2 * rows * depth + 4 * rows * columns,
             transcendentals=0,
         ),
-        input_output_aliases={} if held is None else {count + 2: 0},
         name="base",
-    )(places, *pieces, weight, *extra)
-
-
-def last_kernel(spare, begins, base, shrunk, low, high, out, spread):
+    )(*pieces, weight)
+
+
+def last_kernel(spare, shard, scalars, *refs):
+    bases = refs[:2]
+    shrunk, low, high, out, spread, lora = refs[2:]
     width, tiles, height = low.shape[0], low.shape[1], low.shape[2]
     inner, others = width * height, high.shape[2]
 
@@ -186,7 +172,7 @@
         for s in range(width):
             both = jnp.concatenate([shrunk[s, i] for i in range(spare)], axis=0)[:half]
             for h in range(2):
-                rows = pl.ds(pl.multiple_of(begins[s] + h * half, BLOCK), half)
+                rows = pl.ds(pl.multiple_of(scalars[s] + h * half, BLOCK), half)
                 mine = both[:, h * half : (h + 1) * half]
                 spread[rows, s * height : (s + 1) * height] = mine[:, :height]
                 spread[rows, inner + s * others : inner + (s + 1) * others] = mine[:, height:]
@@ -198,30 +184,40 @@
         ],
         axis=0,
     )
-    lora = jnp.dot(spread[...], expand, preferred_element_type=jnp.float32).astype(jnp.bfloat16)
-    out[...] = (base[...] + lora.astype(jnp.float32)).astype(jnp.bfloat16)
-
-
-def last(begins, base, low, high, spare):
-    total_rows, columns = base.shape
+    lora[...] = jnp.dot(spread[...], expand, preferred_element_type=jnp.float32)
+    i = width
+    for base in bases:
+        for at in range(0, base.shape[0], shard):
+            rows = pl.ds(pl.multiple_of(scalars[i], shard), shard)
+            rounded = lora[rows, :].astype(jnp.bfloat16).astype(jnp.float32)
+            out[rows, :] = (base[at : at + shard] + rounded).astype(jnp.bfloat16)
+            i += 1
+
+
+def last(scalars, bases, low, high, spare, shard):
+    total_rows, columns = sum(b.shape[0] for b in bases), bases[0].shape[1]
     width, all_tiles, height, _ = low.shape
     others = high.shape[2]
     tiles = 2 if all_tiles % 2 == 0 and spare % 2 == 0 else 1
     tile = tiles * LANES
     return pl.pallas_call(
-        functools.partial(last_kernel, spare),
+        functools.partial(last_kernel, spare, shard),
         out_shape=jax.ShapeDtypeStruct((total_rows, columns), jnp.bfloat16),
         grid_spec=pltpu.PrefetchScalarGridSpec(
             num_scalar_prefetch=1,
             grid=(columns // tile,),
             in_specs=[
-                pl.BlockSpec((total_rows, tile), lambda n, s: (0, n)),
+                pl.BlockSpec((bases[0].shape[0], tile), lambda n, s: (0, n)),
+                pl.BlockSpec((bases[1].shape[0], tile), lambda n, s: (0, n)),
                 pl.BlockSpec((width, spare, others, LANES), lambda n, s: (0, 0, 0, 0)),
                 pl.BlockSpec((width, tiles, height, LANES), lambda n, s: (0, n, 0, 0)),
                 pl.BlockSpec((width, tiles, others, LANES), lambda n, s: (0, n + spare // tiles, 0, 0)),
             ],
             out_specs=pl.BlockSpec((total_rows, tile), lambda n, s: (0, n)),
-            scratch_shapes=[pltpu.VMEM((total_rows, width * (height + others)), jnp.bfloat16)],
+            scratch_shapes=[
+                pltpu.VMEM((total_rows, width * (height + others)), jnp.bfloat16),
+                pltpu.VMEM((total_rows, tile), jnp.float32),
+            ],
         ),
         compiler_params=pltpu.CompilerParams(vmem_limit_bytes=VMEM_LIMIT),
         cost_estimate=pl.CostEstimate(
@@ -230,7 +226,7 @@
             transcendentals=0,
         ),
         name="last",
-    )(begins, base, high, low, high)
+    )(scalars, *bases, high, low, high)
 
 
 def local(tokens, gate_weight, adapter_shrink, adapter_expand, adapter_blocks, adapter_position):
@@ -240,9 +236,8 @@
     columns = gate_weight.shape[1]
     rank = adapter_shrink.shape[2]
     total_rows = shard * width
-    chips = width // 2
-    chip_rows = 2 * shard
-    chip, core = me // 2, me % 2
+    planes = width // 4
+    z, y, core = me // 4, (me // 2) % 2, me % 2
 
     count = adapter_position.shape[0]
     ids = jnp.arange(count, dtype=jnp.int32)
@@ -254,68 +249,65 @@
     size_by_slot = jnp.sum(jnp.where(at_slot, sizes[None, :], 0), axis=1)
     begin_by_slot = jnp.minimum(start_by_slot, total_rows - capacity)
 
-    ring = list(range(0, chips, 2)) + list(range(chips - 1, 0, -2))
-    place = [ring.index(a) for a in range(chips)]
-    swap_core = [(a * 2 + c, a * 2 + 1 - c) for a in range(chips) for c in range(2)]
-    around = [
-        (a * 2 + c, ring[(place[a] + 1 - 2 * c) % chips] * 2 + c) for a in range(chips) for c in range(2)
-    ]
-    behind = jnp.asarray([[ring[(place[a] - j) % chips] for j in range(chips)] for a in range(chips)], jnp.int32)
-    behind = lax.dynamic_index_in_dim(behind, chip, 0, keepdims=False)
+    def at(z_, y_, core_):
+        return (z_ * 2 + y_) * 2 + core_
+
+    both = [(a, b, c) for a in range(planes) for b in range(2) for c in range(2)]
+    swap_core = [(at(a, b, c), at(a, b, 1 - c)) for a, b, c in both]
+    swap_y = [(at(a, b, c), at(a, 1 - b, c)) for a, b, c in both]
+    ring = [0] + list(range(1, planes, 2)) + list(range((planes - 1) // 2 * 2, 0, -2))
+    place = [ring.index(a) for a in range(planes)]
+    around = [(at(a, b, c), at(ring[(place[a] + 1) % planes], b, c)) for a, b, c in both]
+    origin = jnp.asarray([[ring[(place[a] - j) % planes] for j in range(planes)] for a in range(planes)], jnp.int32)
+    origin = lax.dynamic_index_in_dim(origin, z, 0, keepdims=False)
 
     def send(value, pairs):
         return lax.ppermute(value, AXIS, pairs)
 
     shrink_t = jnp.swapaxes(adapter_shrink[0], 0, 1)
-    height = rank // 2
+    height = 3 * rank // 4
     spare = -(-(MOST * BLOCK // 2) // (rank - height))
 
     low, high = parts_of(adapter_expand[0], height, width, spare)
-    half_way = chips // 2
-    first = send(tokens, around)
-    neighbour = send(tokens, swap_core)
-    second = send(neighbour, around)
-    pieces = [tokens, neighbour]
-    places = [me * shard, (chip * 2 + 1 - core) * shard]
-    swapped = [neighbour]
-    for j in range(1, half_way + 1):
-        mine_from = jnp.where(core == 0, behind[j], behind[chips - j]) * 2
-        other_from = jnp.where(core == 0, behind[chips - j], behind[j]) * 2
-        if j < half_way:
-            first, second = order([first, second], swapped + [low, high])
-            next_first = send(first, around)
-            next_second = send(second, around) if j + 1 < half_way else None
-            swapped = [send(first, swap_core), send(second, swap_core)]
-            pieces += [first, second] + swapped
-            places += [
-                (mine_from + core) * shard,
-                (mine_from + 1 - core) * shard,
-                (other_from + 1 - core) * shard,
-                (other_from + core) * shard,
-            ]
-            first, second = next_first, next_second
+    coming, across = send(tokens, around), send(tokens, swap_y)
+    mine, mine_other = tokens, send(tokens, swap_core)
+    before = [low, high]
+    pieces, places, bases = [], [], []
+    some = 2 * planes
+    for j in range(planes):
+        last_one = j == planes - 1
+        if not last_one:
+            coming, across = order([coming, across], before)
+            onward = send(coming, around) if j + 2 < planes else None
+            onward_across = send(coming, swap_y)
+            coming_other = send(coming, swap_core)
         else:
-            low = order([low], [first] + swapped)[0]
-            swapped.append(send(first, swap_core))
+            across = order([across], bases)[0]
+        across_other = send(across, swap_core)
+        before = [across_other] if last_one else [coming_other, across_other]
+        if j + 2 == planes:
+            low = order([low], [coming])[0]
             low = lax.all_to_all(low, AXIS, split_axis=0, concat_axis=0, tiled=True)
-            pieces += [first, swapped[-1]]
-            places += [(mine_from + core) * shard, (other_from + 1 - core) * shard]
+            arrays = pieces[:some]
+            arrays = order(arrays, [coming])
+            bases.append(base_matmul(arrays, gate_weight, 4))
+        pieces += [mine, across, mine_other, across_other]
+        for core_ in (core, 1 - core):
+            for y_ in (y, 1 - y):
+                places.append(((origin[j] * 2 + y_) * 2 + core_) * shard)
+        if not last_one:
+            mine, mine_other, coming, across = coming, coming_other, onward, onward_across
     places = jnp.stack(places).astype(jnp.int32)
 
     mine = jnp.stack([begin_by_slot[me], start_by_slot[me], size_by_slot[me]])
     scalars = jnp.concatenate([places, mine]).astype(jnp.int32)
     high = shrink_rows(scalars, pieces, shrink_t, high, spare)
-    tile = 256
-    while columns % tile or total_rows * tile > 1024 * 256:
-        tile //= 2
-    steps = columns // tile
-    early = max(steps // 7, 1)
-    places = order([places], [high])[0]
-    base = base_matmul(places, pieces, gate_weight, None, 0, early, tile)
-    high, base, places = order([high, base, places], [low])
+    high = order([high], [low])[0]
+    arrays = order(pieces[some:], [high])
     high = lax.all_to_all(high, AXIS, split_axis=0, concat_axis=0, tiled=True)
-    base = base_matmul(places, pieces, gate_weight, base, early, steps - early, tile)
-    return last(begin_by_slot.astype(jnp.int32), base, low, high, spare)
+    bases.append(base_matmul(arrays, gate_weight))
+    scalars = jnp.concatenate([begin_by_slot.astype(jnp.int32), places])
+    return last(scalars, bases, low, high, spare, shard)
 
 
 def solution(mesh):

time: 209 us -> 196 us (0.938)
  Pallas kernels: 75.9 us -> 67.6 us
  starting transfers between devices: 25.4 us -> 31.3 us
  between operations: 8.17 us -> 2.73 us
  local copies, waits for them, and re-layouts: 10.9 us -> 6.4 us
    all_to_all x1, waiting for transfers between devices: 5.07 us -> 23.2 us  [local(): low = lax.all_to_all(low, AXIS, split_axis=0, concat_axis=0, tiled=True)]
    ppermute x15, waiting for transfers between devices: 75 us -> 59.7 us  [send(): return lax.ppermute(value, AXIS, pairs)]
    pallas_call x2, Pallas kernels: 55.8 us -> 46.9 us  [base_matmul(): pl.pallas_call(functools.partial(base_kernel, count), out_shape=jax.Shape...]
    ppermute x15, starting transfers between devices: 13.7 us -> 19.3 us  [send(): return lax.ppermute(value, AXIS, pairs)]
    unnamed x38 -> x24, local copies, waits for them, and re-layouts: 4.66 us -> 0.05 us
    all_to_all x1, waiting for transfers between devices: 7.99 us -> 3.78 us  [local(): high = lax.all_to_all(high, AXIS, split_axis=0, concat_axis=0, tiled=True)]
  transfers between devices with their start and end apart: 17 -> 17, of which waited for: 11 -> 9; matrix products, arithmetic and copies ran while one was open for 3% -> 3% of each run, Pallas kernels for 31% -> 29%
where the time goes in v4:
time: 196 us; the launch traced here: 195 us
  waiting for transfers between devices  86.6 us (44%)
  Pallas kernels  67.6 us (34%)
  starting transfers between devices  31.3 us (16%)
  local copies, waits for them, and re-layouts  6.4 us (3%)
  between operations  2.73 us (1%)
    ppermute x15, waiting for transfers between devices, send(): return lax.ppermute(value, AXIS, pairs)  59.7 us
    pallas_call x2, Pallas kernels, base_matmul(): pl.pallas_call(functools.partial(base_kernel, count), out_shape=jax.Shape...  46.9 us
    all_to_all x1, waiting for transfers between devices, local(): low = lax.all_to_all(low, AXIS, split_axis=0, concat_axis=0, tiled=True)  23.2 us
    ppermute x15, starting transfers between devices, send(): return lax.ppermute(value, AXIS, pairs)  19.3 us
    pallas_call x1, Pallas kernels, last(): pl.pallas_call(functools.partial(last_kernel, spare, shard), out_shape=ja...  11.5 us
    all_to_all x1, starting transfers between devices, local(): low = lax.all_to_all(low, AXIS, split_axis=0, concat_axis=0, tiled=True)  7.14 us
    all_to_all x1, starting transfers between devices, local(): high = lax.all_to_all(high, AXIS, split_axis=0, concat_axis=0, tiled=True)  4.91 us
    pallas_call x1, Pallas kernels, parts_of(): pl.pallas_call(parts_kernel, out_shape=[jax.ShapeDtypeStruct((width, tile...  4.68 us
  transfers between devices with their start and end apart: 17, of which 9 were waited for; matrix products, arithmetic and copies ran while one was open for 3% of the time, Pallas kernels for 29%

profile of v4, /device:TPU:13, one launch (start us, length us, event | category | flops | bytes accessed | tf_op | source)
XLA Modules:
  0.0 194.9 jit_solution(5708696385076073744)
XLA Ops:
  0.2 2.3 %collective-permute-start = (bf16[64,8192]{1,0:T(8,128)(2,1)}, bf16[64,8192]{1,0:T(8,128)(2,1)S(1)}, u32[]{:S(2)}, u32[]{:S(2)}) collective-permute-start(bf16[64,8192]{1,0:T(8,128)(2,1)} %refs_0_.2), channel_id=1, source_target_pairs={{0,4},{1,5},{2,6},{3,7},{4,12},{5,13},{6,14},{7,15},{8,0},{9,1},{1... | collective-permute-start | bytes 3145736 | tf_op jit(solution)/shard_map/ppermute | solution.py:265
  2.5 4.7 %parts.1 = (bf16[16,14,48,128]{3,2,1,0:T(8,128)(2,1)}, bf16[16,18,16,128]{3,2,1,0:T(8,128)(2,1)}) custom-call(bf16[64,28672]{1,0:T(8,128)(2,1)} %bitcast.24), custom_call_target="tpu_custom_call" | custom-call | bytes 7340032 | tf_op jit(solution)/shard_map/parts/pallas_call | solution.py:35
  7.2 17.0 %collective-permute-done.1.refs_1_ = bf16[64,8192]{1,0:T(8,128)(2,1)S(1)} collective-permute-done((bf16[64,8192]{1,0:T(8,128)(2,1)}, bf16[64,8192]{1,0:T(8,128)(2,1)S(1)}, u32[]{:S(2)}, u32[]{:S(2)}) %collective-permute-start.1) | collective-permute-done | bytes 1048608 | tf_op jit(solution)/shard_map/ppermute | solution.py:265
  24.4 1.9 collective-permute-start.3
  26.2 1.2 collective-permute-start.5
  27.5 3.0 %collective-permute-start.4 = (bf16[64,8192]{1,0:T(8,128)(2,1)S(1)}, bf16[64,8192]{1,0:T(8,128)(2,1)S(1)}, u32[]{:S(2)}, u32[]{:S(2)}) collective-permute-start(bf16[64,8192]{1,0:T(8,128)(2,1)S(1)} %collective-permute-done.refs_4_), channel_id=1, source_target_pairs={{0,4},{1,5},{2,6},{3,7},{4,12},{5,13},{6,14},{7,15},{8,0},{9,1},{1... | collective-permute-start | bytes 3145736 | tf_op jit(solution)/shard_map/ppermute | solution.py:265
  30.5 20.0 %collective-permute-done.5.refs_5_ = bf16[64,8192]{1,0:T(8,128)(2,1)S(1)} collective-permute-done((bf16[64,8192]{1,0:T(8,128)(2,1)S(1)}, bf16[64,8192]{1,0:T(8,128)(2,1)S(1)}, u32[]{:S(2)}, u32[]{:S(2)}) %collective-permute-start.5) | collective-permute-done | bytes 1048608 | tf_op jit(solution)/shard_map/ppermute | solution.py:265
  50.5 1.7 collective-permute-done.4.refs_8_.refs_0_
  52.2 1.7 collective-permute-start.7
  54.1 3.2 %collective-permute-start.8 = (bf16[64,8192]{1,0:T(8,128)(2,1)S(1)}, bf16[64,8192]{1,0:T(8,128)(2,1)}, u32[]{:S(2)}, u32[]{:S(2)}) collective-permute-start(bf16[64,8192]{1,0:T(8,128)(2,1)S(1)} %collective-permute-done.4.refs_8_.refs_0_), channel_id=1, source_target_pairs={{0,4},{1,5},{2,6},{3,7},{4,12},{5,13},{6,14},{7,15},{8,0},{9,1},{1... | collective-permute-start | bytes 3145736 | tf_op jit(solution)/shard_map/ppermute | solution.py:265
  57.2 1.0 collective-permute-start.2
  58.3 19.9 %collective-permute-done.9.refs_9_.refs_1_ = bf16[64,8192]{1,0:T(8,128)(2,1)} collective-permute-done((bf16[64,8192]{1,0:T(8,128)(2,1)S(1)}, bf16[64,8192]{1,0:T(8,128)(2,1)}, u32[]{:S(2)}, u32[]{:S(2)}) %collective-permute-start.9) | collective-permute-done | bytes 1048608 | tf_op jit(solution)/shard_map/ppermute | solution.py:265
  78.2 0.8 collective-permute-done.8.refs_12_.refs_4_
  79.0 1.6 collective-permute-start.13
  80.6 1.2 collective-permute-start.12
  81.9 7.1 %all-to-all-start = ((bf16[16,14,48,128]{3,2,1,0:T(8,128)(2,1)}), bf16[16,14,48,128]{3,2,1,0:T(8,128)(2,1)S(1)}, u32[]{:S(2)}, u32[]{:S(2)}) async-start(bf16[16,14,48,128]{3,2,1,0:T(8,128)(2,1)} %get-tuple-element.49), calls=%async_computation | async-start | bytes 5505024 | tf_op jit(solution)/shard_map/all_to_all | solution.py:290
  89.1 0.4 collective-permute-start.11
  89.5 23.5 %base.2.refs_0_ = f32[512,1792]{1,0:T(8,128)} custom-call(bf16[64,8192]{1,0:T(8,128)(2,1)} %refs_0_.2, bf16[64,8192]{1,0:T(8,128)(2,1)} %copy-done.3, bf16[64,8192]{1,0:T(8,128)(2,1)} %collective-permute-done.2.refs_2_, bf16[64,8192]{1,0:T(8,128)(2,1)} %copy-done.6, bf16[64,8192]{1,0:T(8,128)(2,1)} %copy-done.4, bf16[64,8192]{1,0:T(8,128)(2,1)} %copy-done.8, ...), custom_call_target="tpu_custom_call" | custom-call | flops 60129542144 | bytes 41418752 | tf_op jit(solution)/shard_map/base/pallas_call | solution.py:145
  113.0 1.3 collective-permute-start.14
  114.3 0.7 constant_dynamic-slice_fusion
  115.0 0.7 fusion
  118.5 0.7 dynamic_slice.15
  119.2 0.6 dynamic_slice.16
  119.8 0.6 dynamic_slice.14
  120.4 2.5 %concatenate.9.scalars = s32[19]{0:T(128)} concatenate(s32[1]{0:T(128)} %bitcast.1, s32[1]{0:T(128)} %bitcast.2, s32[1]{0:T(128)} %bitcast.3, s32[1]{0:T(128)} %bitcast.4, s32[1]{0:T(128)} %bitcast.6, s32[1]{0:T(128)} %bitcast.7, s32[1]{0:T(128)} %bitcast.8, s32[1]{0:T(128)} %bitcast.9, s32[1]{0:T(128)} %bitcast.11, s32[1]{0:T(128)} %bitcast.12, s32[1]{0:T(128)} %bitcast.13, ...), dimensions={0} | concatenate | bytes 152 | tf_op jit(solution)/shard_map/concatenate | solution.py:303
  122.9 4.5 %shrink.1 = bf16[16,18,16,128]{3,2,1,0:T(8,128)(2,1)} custom-call(s32[19]{0:T(128)} %concatenate.9.scalars, bf16[64,8192]{1,0:T(8,128)(2,1)} %refs_0_.2, bf16[64,8192]{1,0:T(8,128)(2,1)} %copy-done.3, bf16[64,8192]{1,0:T(8,128)(2,1)} %collective-permute-done.2.refs_2_, bf16[64,8192]{1,0:T(8,128)(2,1)} %copy-done.6, ...), custom_call_target="tpu_custom_call", output_to_operand_aliasing={{}: (18, {})} | custom-call | flops 134217728 | bytes 2097152 | tf_op jit(solution)/shard_map/shrink/pallas_call | solution.py:99
  127.4 23.2 %all-to-all-done.refs_3_ = bf16[16,14,48,128]{3,2,1,0:T(8,128)(2,1)S(1)} async-done(((bf16[16,14,48,128]{3,2,1,0:T(8,128)(2,1)}), bf16[16,14,48,128]{3,2,1,0:T(8,128)(2,1)S(1)}, u32[]{:S(2)}, u32[]{:S(2)}) %all-to-all-start) | async-done | bytes 2752544 | tf_op jit(solution)/shard_map/all_to_all | solution.py:290
  150.6 4.9 %all-to-all-start.1 = ((bf16[16,18,16,128]{3,2,1,0:T(8,128)(2,1)}), bf16[16,18,16,128]{3,2,1,0:T(8,128)(2,1)}, u32[]{:S(2)}, u32[]{:S(2)}) async-start(bf16[16,18,16,128]{3,2,1,0:T(8,128)(2,1)} %shrink.1), calls=%async_computation.1 | async-start | bytes 2359296 | tf_op jit(solution)/shard_map/all_to_all | solution.py:307
  155.5 0.6 concatenate.8.scalars
  156.1 23.4 %base.3.refs_1_ = f32[512,1792]{1,0:T(8,128)} custom-call(bf16[64,8192]{1,0:T(8,128)(2,1)} %copy-done.2, bf16[64,8192]{1,0:T(8,128)(2,1)} %collective-permute-done.9.refs_9_.refs_1_, bf16[64,8192]{1,0:T(8,128)(2,1)} %copy-done.5, bf16[64,8192]{1,0:T(8,128)(2,1)} %collective-permute-done.11.refs_11_.refs_3_, ...), custom_call_target="tpu_custom_call" | custom-call | flops 15032385536 | bytes 41418752 | tf_op jit(solution)/shard_map/base/pallas_call | solution.py:145
  179.6 3.8 %all-to-all-done.1.refs_2_.refs_4_ = bf16[16,18,16,128]{3,2,1,0:T(8,128)(2,1)} async-done(((bf16[16,18,16,128]{3,2,1,0:T(8,128)(2,1)}), bf16[16,18,16,128]{3,2,1,0:T(8,128)(2,1)}, u32[]{:S(2)}, u32[]{:S(2)}) %all-to-all-start.1) | async-done | bytes 1179680 | tf_op jit(solution)/shard_map/all_to_all | solution.py:307
  183.4 11.5 %last.1 = bf16[1024,1792]{1,0:T(8,128)(2,1)} custom-call(s32[32]{0:T(128)} %concatenate.8.scalars, f32[512,1792]{1,0:T(8,128)} %base.2.refs_0_, f32[512,1792]{1,0:T(8,128)} %base.3.refs_1_, bf16[16,18,16,128]{3,2,1,0:T(8,128)(2,1)} %all-to-all-done.1.refs_2_.refs_4_, bf16[16,14,48,128]{3,2,1,0:T(8,128)(2,1)} %copy-done, ...), custom_call_target="tpu_custom_call" | custom-call | flops 3758096384 | bytes 14680064 | tf_op jit(solution)/shard_map/last/pallas_call | solution.py:203
  (42 shorter events, 1.0 us)
Async XLA Ops:
  0.0 57.2 %copy-start.1 = (bf16[64,8192]{1,0:T(8,128)(2,1)S(1)}, bf16[64,8192]{1,0:T(8,128)(2,1)}, u32[]{:S(2)}) copy-start(bf16[64,8192]{1,0:T(8,128)(2,1)} %refs_0_.2) | copy-start | bytes 3145732
  0.0 24.2 %collective-permute-start.1 = (bf16[64,8192]{1,0:T(8,128)(2,1)}, bf16[64,8192]{1,0:T(8,128)(2,1)S(1)}, u32[]{:S(2)}, u32[]{:S(2)}) collective-permute-start(bf16[64,8192]{1,0:T(8,128)(2,1)} %refs_0_.2), channel_id=1, source_target_pairs={{0,2},{1,3},{2,0},{3,1},{4,6},{5,7},{6,4},{7,5},{8,10},{9,11},{10,... | collective-permute-start | bytes 3145736 | tf_op jit(solution)/shard_map/ppermute | solution.py:265
  0.2 24.1 %collective-permute-start = (bf16[64,8192]{1,0:T(8,128)(2,1)}, bf16[64,8192]{1,0:T(8,128)(2,1)S(1)}, u32[]{:S(2)}, u32[]{:S(2)}) collective-permute-start(bf16[64,8192]{1,0:T(8,128)(2,1)} %refs_0_.2), channel_id=1, source_target_pairs={{0,4},{1,5},{2,6},{3,7},{4,12},{5,13},{6,14},{7,15},{8,0},{9,1},{1... | collective-permute-start | bytes 3145736 | tf_op jit(solution)/shard_map/ppermute | solution.py:265
  24.2 54.8 %copy-start.3 = (bf16[64,8192]{1,0:T(8,128)(2,1)}, bf16[64,8192]{1,0:T(8,128)(2,1)S(1)}, u32[]{:S(2)}) copy-start(bf16[64,8192]{1,0:T(8,128)(2,1)S(1)} %collective-permute-done.1.refs_1_) | copy-start | bytes 3145732
  24.4 56.3 %copy-start.4 = (bf16[64,8192]{1,0:T(8,128)(2,1)}, bf16[64,8192]{1,0:T(8,128)(2,1)S(1)}, u32[]{:S(2)}) copy-start(bf16[64,8192]{1,0:T(8,128)(2,1)S(1)} %collective-permute-done.refs_4_) | copy-start | bytes 3145732
  24.4 6.1 %collective-permute-start.3 = (bf16[64,8192]{1,0:T(8,128)(2,1)S(1)}, bf16[64,8192]{1,0:T(8,128)(2,1)S(1)}, u32[]{:S(2)}, u32[]{:S(2)}) collective-permute-start(bf16[64,8192]{1,0:T(8,128)(2,1)S(1)} %collective-permute-done.1.refs_1_), channel_id=1, source_target_pairs={{0,1},{1,0},{2,3},{3,2},{4,5},{5,4},{6,7},{7,6},{8,9},{9,8},{10,11... | collective-permute-start | bytes 3145736 | tf_op jit(solution)/shard_map/ppermute | solution.py:265
  26.2 4.2 %collective-permute-start.6 = (bf16[64,8192]{1,0:T(8,128)(2,1)S(1)}, bf16[64,8192]{1,0:T(8,128)(2,1)S(1)}, u32[]{:S(2)}, u32[]{:S(2)}) collective-permute-start(bf16[64,8192]{1,0:T(8,128)(2,1)S(1)} %collective-permute-done.refs_4_), channel_id=1, source_target_pairs={{0,1},{1,0},{2,3},{3,2},{4,5},{5,4},{6,7},{7,6},{8,9},{9,8},{10,11... | collective-permute-start | bytes 3145736 | tf_op jit(solution)/shard_map/ppermute | solution.py:265
  26.2 24.2 %collective-permute-start.5 = (bf16[64,8192]{1,0:T(8,128)(2,1)S(1)}, bf16[64,8192]{1,0:T(8,128)(2,1)S(1)}, u32[]{:S(2)}, u32[]{:S(2)}) collective-permute-start(bf16[64,8192]{1,0:T(8,128)(2,1)S(1)} %collective-permute-done.refs_4_), channel_id=1, source_target_pairs={{0,2},{1,3},{2,0},{3,1},{4,6},{5,7},{6,4},{7,5},{8,10},{9,11},{10,... | collective-permute-start | bytes 3145736 | tf_op jit(solution)/shard_map/ppermute | solution.py:265
  27.5 24.7 %collective-permute-start.4 = (bf16[64,8192]{1,0:T(8,128)(2,1)S(1)}, bf16[64,8192]{1,0:T(8,128)(2,1)S(1)}, u32[]{:S(2)}, u32[]{:S(2)}) collective-permute-start(bf16[64,8192]{1,0:T(8,128)(2,1)S(1)} %collective-permute-done.refs_4_), channel_id=1, source_target_pairs={{0,4},{1,5},{2,6},{3,7},{4,12},{5,13},{6,14},{7,15},{8,0},{9,1},{1... | collective-permute-start | bytes 3145736 | tf_op jit(solution)/shard_map/ppermute | solution.py:265
  30.5 21.7 %copy-start.6 = (bf16[64,8192]{1,0:T(8,128)(2,1)}, bf16[64,8192]{1,0:T(8,128)(2,1)S(1)}, u32[]{:S(2)}) copy-start(bf16[64,8192]{1,0:T(8,128)(2,1)S(1)} %collective-permute-done.3.refs_3_) | copy-start | bytes 3145732
  30.5 51.4 %copy-start.7 = (bf16[64,8192]{1,0:T(8,128)(2,1)}, bf16[64,8192]{1,0:T(8,128)(2,1)S(1)}, u32[]{:S(2)}) copy-start(bf16[64,8192]{1,0:T(8,128)(2,1)S(1)} %collective-permute-done.6.refs_6_) | copy-start | bytes 3145732
  50.4 31.4 %copy-start.8 = (bf16[64,8192]{1,0:T(8,128)(2,1)}, bf16[64,8192]{1,0:T(8,128)(2,1)S(1)}, u32[]{:S(2)}) copy-start(bf16[64,8192]{1,0:T(8,128)(2,1)S(1)} %collective-permute-done.5.refs_5_) | copy-start | bytes 3145732
  52.2 29.7 %copy-start.2 = (bf16[64,8192]{1,0:T(8,128)(2,1)}, bf16[64,8192]{1,0:T(8,128)(2,1)S(1)}, u32[]{:S(2)}) copy-start(bf16[64,8192]{1,0:T(8,128)(2,1)S(1)} %collective-permute-done.4.refs_8_.refs_0_) | copy-start | bytes 3145732
  52.2 6.1 %collective-permute-start.7 = (bf16[64,8192]{1,0:T(8,128)(2,1)S(1)}, bf16[64,8192]{1,0:T(8,128)(2,1)S(1)}, u32[]{:S(2)}, u32[]{:S(2)}) collective-permute-start(bf16[64,8192]{1,0:T(8,128)(2,1)S(1)} %collective-permute-done.5.refs_5_), channel_id=1, source_target_pairs={{0,1},{1,0},{2,3},{3,2},{4,5},{5,4},{6,7},{7,6},{8,9},{9,8},{10,11... | collective-permute-start | bytes 3145736 | tf_op jit(solution)/shard_map/ppermute | solution.py:265
  53.8 4.4 %collective-permute-start.10 = (bf16[64,8192]{1,0:T(8,128)(2,1)S(1)}, bf16[64,8192]{1,0:T(8,128)(2,1)S(1)}, u32[]{:S(2)}, u32[]{:S(2)}) collective-permute-start(bf16[64,8192]{1,0:T(8,128)(2,1)S(1)} %collective-permute-done.4.refs_8_.refs_0_), channel_id=1, source_target_pairs={{0,1},{1,0},{2,3},{3,2},{4,5},{5,4},{6,7},{7,6},{8,9},{9,8},{10,11... | collective-permute-start | bytes 3145736 | tf_op jit(solution)/shard_map/ppermute | solution.py:265
  53.9 24.3 %collective-permute-start.9 = (bf16[64,8192]{1,0:T(8,128)(2,1)S(1)}, bf16[64,8192]{1,0:T(8,128)(2,1)}, u32[]{:S(2)}, u32[]{:S(2)}) collective-permute-start(bf16[64,8192]{1,0:T(8,128)(2,1)S(1)} %collective-permute-done.4.refs_8_.refs_0_), channel_id=1, source_target_pairs={{0,2},{1,3},{2,0},{3,1},{4,6},{5,7},{6,4},{7,5},{8,10},{9,11},{10,... | collective-permute-start | bytes 3145736 | tf_op jit(solution)/shard_map/ppermute | solution.py:265
  54.1 24.9 %collective-permute-start.8 = (bf16[64,8192]{1,0:T(8,128)(2,1)S(1)}, bf16[64,8192]{1,0:T(8,128)(2,1)}, u32[]{:S(2)}, u32[]{:S(2)}) collective-permute-start(bf16[64,8192]{1,0:T(8,128)(2,1)S(1)} %collective-permute-done.4.refs_8_.refs_0_), channel_id=1, source_target_pairs={{0,4},{1,5},{2,6},{3,7},{4,12},{5,13},{6,14},{7,15},{8,0},{9,1},{1... | collective-permute-start | bytes 3145736 | tf_op jit(solution)/shard_map/ppermute | solution.py:265
  57.2 24.6 %collective-permute-start.2 = (bf16[64,8192]{1,0:T(8,128)(2,1)S(1)}, bf16[64,8192]{1,0:T(8,128)(2,1)}, u32[]{:S(2)}, u32[]{:S(2)}) collective-permute-start(bf16[64,8192]{1,0:T(8,128)(2,1)S(1)} %copy-done.1), channel_id=1, source_target_pairs={{0,1},{1,0},{2,3},{3,2},{4,5},{5,4},{6,7},{7,6},{8,9},{9,8},{10,11... | collective-permute-start | bytes 3145736 | tf_op jit(solution)/shard_map/ppermute | solution.py:265
  58.3 23.6 %copy-start.9 = (bf16[64,8192]{1,0:T(8,128)(2,1)}, bf16[64,8192]{1,0:T(8,128)(2,1)S(1)}, u32[]{:S(2)}) copy-start(bf16[64,8192]{1,0:T(8,128)(2,1)S(1)} %collective-permute-done.7.refs_7_) | copy-start | bytes 3145732
  58.3 23.6 %copy-start.5 = (bf16[64,8192]{1,0:T(8,128)(2,1)}, bf16[64,8192]{1,0:T(8,128)(2,1)S(1)}, u32[]{:S(2)}) copy-start(bf16[64,8192]{1,0:T(8,128)(2,1)S(1)} %collective-permute-done.10.refs_10_.refs_2_) | copy-start | bytes 3145732
  79.0 43.9 %collective-permute-start.13 = (bf16[64,8192]{1,0:T(8,128)(2,1)}, bf16[64,8192]{1,0:T(8,128)(2,1)}, u32[]{:S(2)}, u32[]{:S(2)}) collective-permute-start(bf16[64,8192]{1,0:T(8,128)(2,1)} %collective-permute-done.8.refs_12_.refs_4_), channel_id=1, source_target_pairs={{0,1},{1,0},{2,3},{3,2},{4,5},{5,4},{6,7},{7,6},{8,9},{9,8},{10,11... | collective-permute-start | bytes 3145736 | tf_op jit(solution)/shard_map/ppermute | solution.py:265
  80.6 32.4 %collective-permute-start.12 = (bf16[64,8192]{1,0:T(8,128)(2,1)}, bf16[64,8192]{1,0:T(8,128)(2,1)}, u32[]{:S(2)}, u32[]{:S(2)}) collective-permute-start(bf16[64,8192]{1,0:T(8,128)(2,1)} %collective-permute-done.8.refs_12_.refs_4_), channel_id=1, source_target_pairs={{0,2},{1,3},{2,0},{3,1},{4,6},{5,7},{6,4},{7,5},{8,10},{9,11},{10,... | collective-permute-start | bytes 3145736 | tf_op jit(solution)/shard_map/ppermute | solution.py:265
  81.9 68.7 %all-to-all-start = ((bf16[16,14,48,128]{3,2,1,0:T(8,128)(2,1)}), bf16[16,14,48,128]{3,2,1,0:T(8,128)(2,1)S(1)}, u32[]{:S(2)}, u32[]{:S(2)}) async-start(bf16[16,14,48,128]{3,2,1,0:T(8,128)(2,1)} %get-tuple-element.49), calls=%async_computation | async-start | bytes 5505024 | tf_op jit(solution)/shard_map/all_to_all | solution.py:290
  89.0 29.2 %copy-start.11 = (s32[16]{0:T(128)S(1)}, s32[16]{0:T(128)}, u32[]{:S(2)}) copy-start(s32[16]{0:T(128)} %param.11) | copy-start | bytes 196
  89.0 29.4 %copy-start.10 = (s32[16]{0:T(128)S(1)}, s32[16]{0:T(128)}, u32[]{:S(2)}) copy-start(s32[16]{0:T(128)} %param.12) | copy-start | bytes 196
  89.1 33.9 %collective-permute-start.11 = (bf16[64,8192]{1,0:T(8,128)(2,1)}, bf16[64,8192]{1,0:T(8,128)(2,1)}, u32[]{:S(2)}, u32[]{:S(2)}) collective-permute-start(bf16[64,8192]{1,0:T(8,128)(2,1)} %collective-permute-done.9.refs_9_.refs_1_), channel_id=1, source_target_pairs={{0,1},{1,0},{2,3},{3,2},{4,5},{5,4},{6,7},{7,6},{8,9},{9,8},{10,11... | collective-permute-start | bytes 3145736 | tf_op jit(solution)/shard_map/ppermute | solution.py:265
  113.0 9.9 %collective-permute-start.14 = (bf16[64,8192]{1,0:T(8,128)(2,1)}, bf16[64,8192]{1,0:T(8,128)(2,1)}, u32[]{:S(2)}, u32[]{:S(2)}) collective-permute-start(bf16[64,8192]{1,0:T(8,128)(2,1)} %collective-permute-done.12.refs_13_.refs_5_), channel_id=1, source_target_pairs={{0,1},{1,0},{2,3},{3,2},{4,5},{5,4},{6,7},{7,6},{8,9},{9,8},{10,11... | collective-permute-start | bytes 3145736 | tf_op jit(solution)/shard_map/ppermute | solution.py:265
  150.6 29.0 %copy-start = (bf16[16,14,48,128]{3,2,1,0:T(8,128)(2,1)}, bf16[16,14,48,128]{3,2,1,0:T(8,128)(2,1)S(1)}, u32[]{:S(2)}) copy-start(bf16[16,14,48,128]{3,2,1,0:T(8,128)(2,1)S(1)} %all-to-all-done.refs_3_) | copy-start | bytes 8257540
  150.6 32.8 %all-to-all-start.1 = ((bf16[16,18,16,128]{3,2,1,0:T(8,128)(2,1)}), bf16[16,18,16,128]{3,2,1,0:T(8,128)(2,1)}, u32[]{:S(2)}, u32[]{:S(2)}) async-start(bf16[16,18,16,128]{3,2,1,0:T(8,128)(2,1)} %shrink.1), calls=%async_computation.1 | async-start | bytes 2359296 | tf_op jit(solution)/shard_map/all_to_all | solution.py:307

commit v5 on v4

--- a/solution.py
+++ b/solution.py
@@ -163,26 +163,24 @@
     bases = refs[:2]
     shrunk, low, high, out, spread, lora = refs[2:]
     width, tiles, height = low.shape[0], low.shape[1], low.shape[2]
-    inner, others = width * height, high.shape[2]
+    rank = height + high.shape[2]
 
     @pl.when(pl.program_id(0) == 0)
     def _():
         spread[...] = jnp.zeros_like(spread)
-        half = LANES // 2
+        half = rank
         for s in range(width):
             both = jnp.concatenate([shrunk[s, i] for i in range(spare)], axis=0)[:half]
             for h in range(2):
                 rows = pl.ds(pl.multiple_of(scalars[s] + h * half, BLOCK), half)
-                mine = both[:, h * half : (h + 1) * half]
-                spread[rows, s * height : (s + 1) * height] = mine[:, :height]
-                spread[rows, inner + s * others : inner + (s + 1) * others] = mine[:, height:]
+                spread[rows, s * rank : (s + 1) * rank] = both[:, h * half : (h + 1) * half]
 
     expand = jnp.concatenate(
         [
-            jnp.concatenate([part[:, t].reshape(width * part.shape[2], LANES) for t in range(tiles)], axis=1)
-            for part in (low, high)
+            jnp.concatenate([low[:, t], high[:, t]], axis=1).reshape(width * rank, LANES)
+            for t in range(tiles)
         ],
-        axis=0,
+        axis=1,
     )
     lora[...] = jnp.dot(spread[...], expand, preferred_element_type=jnp.float32)
     i = width
@@ -271,7 +269,7 @@
     low, high = parts_of(adapter_expand[0], height, width, spare)
     coming, across = send(tokens, around), send(tokens, swap_y)
     mine, mine_other = tokens, send(tokens, swap_core)
-    before = [low, high]
+    before, now = [low, high], []
     pieces, places, bases = [], [], []
     some = 2 * planes
     for j in range(planes):
@@ -284,7 +282,7 @@
         else:
             across = order([across], bases)[0]
         across_other = send(across, swap_core)
-        before = [across_other] if last_one else [coming_other, across_other]
+        before, now = now, [across_other] if last_one else [coming_other, across_other]
         if j + 2 == planes:
             low = order([low], [coming])[0]
             low = lax.all_to_all(low, AXIS, split_axis=0, concat_axis=0, tiled=True)

time: 196 us -> 192 us (0.980)
  waiting for transfers between devices: 86.6 us -> 78.1 us
  starting transfers between devices: 31.3 us -> 35 us
    ppermute x15, waiting for transfers between devices: 59.7 us -> 50.3 us  [send(): return lax.ppermute(value, AXIS, pairs)]
    ppermute x15, starting transfers between devices: 19.3 us -> 23.2 us  [send(): return lax.ppermute(value, AXIS, pairs)]
  transfers between devices with their start and end apart: 17 -> 17, of which waited for: 9 -> 8; matrix products, arithmetic and copies ran while one was open for 3% -> 3% of each run, Pallas kernels for 29% -> 29%
where the time goes in v5:
time: 192 us; the launch traced here: 191 us
  waiting for transfers between devices  78.1 us (41%)
  Pallas kernels  67.3 us (35%)
  starting transfers between devices  35 us (18%)
  local copies, waits for them, and re-layouts  7.43 us (4%)
  between operations  2.67 us (1%)
    ppermute x15, waiting for transfers between devices, send(): return lax.ppermute(value, AXIS, pairs)  50.3 us
    pallas_call x2, Pallas kernels, base_matmul(): pl.pallas_call(functools.partial(base_kernel, count), out_shape=jax.Shape...  47 us
    all_to_all x1, waiting for transfers between devices, local(): low = lax.all_to_all(low, AXIS, split_axis=0, concat_axis=0, tiled=True)  24.1 us
    ppermute x15, starting transfers between devices, send(): return lax.ppermute(value, AXIS, pairs)  23.2 us
    pallas_call x1, Pallas kernels, last(): pl.pallas_call(functools.partial(last_kernel, spare, shard), out_shape=ja...  11.3 us
    all_to_all x1, starting transfers between devices, local(): low = lax.all_to_all(low, AXIS, split_axis=0, concat_axis=0, tiled=True)  6.96 us
    all_to_all x1, starting transfers between devices, local(): high = lax.all_to_all(high, AXIS, split_axis=0, concat_axis=0, tiled=True)  4.9 us
    pallas_call x1, Pallas kernels, parts_of(): pl.pallas_call(parts_kernel, out_shape=[jax.ShapeDtypeStruct((width, tile...  4.68 us
  transfers between devices with their start and end apart: 17, of which 8 were waited for; matrix products, arithmetic and copies ran while one was open for 3% of the time, Pallas kernels for 29%

profile of v5, /device:TPU:13, one launch (start us, length us, event | category | flops | bytes accessed | tf_op | source)
XLA Modules:
  0.0 190.8 jit_solution(18386357972785401073)
XLA Ops:
  0.2 2.3 %collective-permute-start = (bf16[64,8192]{1,0:T(8,128)(2,1)}, bf16[64,8192]{1,0:T(8,128)(2,1)S(1)}, u32[]{:S(2)}, u32[]{:S(2)}) collective-permute-start(bf16[64,8192]{1,0:T(8,128)(2,1)} %refs_0_.2), channel_id=1, source_target_pairs={{0,4},{1,5},{2,6},{3,7},{4,12},{5,13},{6,14},{7,15},{8,0},{9,1},{1... | collective-permute-start | bytes 3145736 | tf_op jit(solution)/shard_map/ppermute | solution.py:263
  2.5 4.7 %parts.1 = (bf16[16,14,48,128]{3,2,1,0:T(8,128)(2,1)}, bf16[16,18,16,128]{3,2,1,0:T(8,128)(2,1)}) custom-call(bf16[64,28672]{1,0:T(8,128)(2,1)} %bitcast.24), custom_call_target="tpu_custom_call" | custom-call | bytes 7340032 | tf_op jit(solution)/shard_map/parts/pallas_call | solution.py:35
  7.2 17.0 %collective-permute-done.1.refs_1_ = bf16[64,8192]{1,0:T(8,128)(2,1)S(1)} collective-permute-done((bf16[64,8192]{1,0:T(8,128)(2,1)}, bf16[64,8192]{1,0:T(8,128)(2,1)S(1)}, u32[]{:S(2)}, u32[]{:S(2)}) %collective-permute-start.1) | collective-permute-done | bytes 1048608 | tf_op jit(solution)/shard_map/ppermute | solution.py:263
  24.4 1.2 collective-permute-start.5
  25.6 3.0 %collective-permute-start.4 = (bf16[64,8192]{1,0:T(8,128)(2,1)S(1)}, bf16[64,8192]{1,0:T(8,128)(2,1)}, u32[]{:S(2)}, u32[]{:S(2)}) collective-permute-start(bf16[64,8192]{1,0:T(8,128)(2,1)S(1)} %collective-permute-done.refs_4_), channel_id=1, source_target_pairs={{0,4},{1,5},{2,6},{3,7},{4,12},{5,13},{6,14},{7,15},{8,0},{9,1},{1... | collective-permute-start | bytes 3145736 | tf_op jit(solution)/shard_map/ppermute | solution.py:263
  28.6 2.4 %collective-permute-start.3 = (bf16[64,8192]{1,0:T(8,128)(2,1)S(1)}, bf16[64,8192]{1,0:T(8,128)(2,1)S(1)}, u32[]{:S(2)}, u32[]{:S(2)}) collective-permute-start(bf16[64,8192]{1,0:T(8,128)(2,1)S(1)} %collective-permute-done.1.refs_1_), channel_id=1, source_target_pairs={{0,1},{1,0},{2,3},{3,2},{4,5},{5,4},{6,7},{7,6},{8,9},{9,8},{10,11... | collective-permute-start | bytes 3145736 | tf_op jit(solution)/shard_map/ppermute | solution.py:263
  31.0 16.2 %collective-permute-done.5.refs_5_ = bf16[64,8192]{1,0:T(8,128)(2,1)S(1)} collective-permute-done((bf16[64,8192]{1,0:T(8,128)(2,1)S(1)}, bf16[64,8192]{1,0:T(8,128)(2,1)S(1)}, u32[]{:S(2)}, u32[]{:S(2)}) %collective-permute-start.5) | collective-permute-done | bytes 1048608 | tf_op jit(solution)/shard_map/ppermute | solution.py:263
  47.3 1.6 collective-permute-done.4.refs_8_.refs_0_
  49.1 3.2 %collective-permute-start.8 = (bf16[64,8192]{1,0:T(8,128)(2,1)}, bf16[64,8192]{1,0:T(8,128)(2,1)}, u32[]{:S(2)}, u32[]{:S(2)}) collective-permute-start(bf16[64,8192]{1,0:T(8,128)(2,1)} %collective-permute-done.4.refs_8_.refs_0_), channel_id=1, source_target_pairs={{0,4},{1,5},{2,6},{3,7},{4,12},{5,13},{6,14},{7,15},{8,0},{9,1},{1... | collective-permute-start | bytes 3145736 | tf_op jit(solution)/shard_map/ppermute | solution.py:263
  52.3 3.6 %collective-permute-start.2 = (bf16[64,8192]{1,0:T(8,128)(2,1)S(1)}, bf16[64,8192]{1,0:T(8,128)(2,1)S(1)}, u32[]{:S(2)}, u32[]{:S(2)}) collective-permute-start(bf16[64,8192]{1,0:T(8,128)(2,1)S(1)} %copy-done.1), channel_id=1, source_target_pairs={{0,1},{1,0},{2,3},{3,2},{4,5},{5,4},{6,7},{7,6},{8,9},{9,8},{10,11... | collective-permute-start | bytes 3145736 | tf_op jit(solution)/shard_map/ppermute | solution.py:263
  56.1 0.4 collective-permute-start.10
  56.5 14.3 %collective-permute-done.9.refs_9_.refs_1_ = bf16[64,8192]{1,0:T(8,128)(2,1)S(1)} collective-permute-done((bf16[64,8192]{1,0:T(8,128)(2,1)}, bf16[64,8192]{1,0:T(8,128)(2,1)S(1)}, u32[]{:S(2)}, u32[]{:S(2)}) %collective-permute-start.9) | collective-permute-done | bytes 1048608 | tf_op jit(solution)/shard_map/ppermute | solution.py:263
  70.8 0.9 collective-permute-done.8.refs_12_.refs_4_
  71.8 4.3 %collective-permute-start.13 = (bf16[64,8192]{1,0:T(8,128)(2,1)}, bf16[64,8192]{1,0:T(8,128)(2,1)}, u32[]{:S(2)}, u32[]{:S(2)}) collective-permute-start(bf16[64,8192]{1,0:T(8,128)(2,1)} %collective-permute-done.8.refs_12_.refs_4_), channel_id=1, source_target_pairs={{0,1},{1,0},{2,3},{3,2},{4,5},{5,4},{6,7},{7,6},{8,9},{9,8},{10,11... | collective-permute-start | bytes 3145736 | tf_op jit(solution)/shard_map/ppermute | solution.py:263
  76.0 1.2 collective-permute-start.12
  77.3 1.0 copy-done.8
  78.3 7.0 %all-to-all-start = ((bf16[16,14,48,128]{3,2,1,0:T(8,128)(2,1)}), bf16[16,14,48,128]{3,2,1,0:T(8,128)(2,1)S(1)}, u32[]{:S(2)}, u32[]{:S(2)}) async-start(bf16[16,14,48,128]{3,2,1,0:T(8,128)(2,1)} %get-tuple-element.49), calls=%async_computation | async-start | bytes 5505024 | tf_op jit(solution)/shard_map/all_to_all | solution.py:288
  85.7 23.5 %base.2.refs_0_ = f32[512,1792]{1,0:T(8,128)} custom-call(bf16[64,8192]{1,0:T(8,128)(2,1)} %refs_0_.2, bf16[64,8192]{1,0:T(8,128)(2,1)} %copy-done.2, bf16[64,8192]{1,0:T(8,128)(2,1)} %copy-done.8, bf16[64,8192]{1,0:T(8,128)(2,1)} %copy-done.6, bf16[64,8192]{1,0:T(8,128)(2,1)} %copy-done.4, bf16[64,8192]{1,0:T(8,128)(2,1)} %copy-done.5, ...), custom_call_target="tpu_custom_call" | custom-call | flops 60129542144 | bytes 41418752 | tf_op jit(solution)/shard_map/base/pallas_call | solution.py:145
  109.2 0.5 collective-permute-start.14
  109.7 0.7 constant_dynamic-slice_fusion
  110.4 0.7 fusion
  113.8 0.6 dynamic_slice.15
  114.5 0.7 dynamic_slice.16
  115.1 0.6 dynamic_slice.14
  115.7 2.5 %concatenate.9.scalars = s32[19]{0:T(128)} concatenate(s32[1]{0:T(128)} %bitcast.1, s32[1]{0:T(128)} %bitcast.2, s32[1]{0:T(128)} %bitcast.3, s32[1]{0:T(128)} %bitcast.4, s32[1]{0:T(128)} %bitcast.6, s32[1]{0:T(128)} %bitcast.7, s32[1]{0:T(128)} %bitcast.8, s32[1]{0:T(128)} %bitcast.9, s32[1]{0:T(128)} %bitcast.11, s32[1]{0:T(128)} %bitcast.12, s32[1]{0:T(128)} %bitcast.13, ...), dimensions={0} | concatenate | bytes 152 | tf_op jit(solution)/shard_map/concatenate | solution.py:301
  118.2 4.5 %shrink.1 = bf16[16,18,16,128]{3,2,1,0:T(8,128)(2,1)} custom-call(s32[19]{0:T(128)} %concatenate.9.scalars, bf16[64,8192]{1,0:T(8,128)(2,1)} %refs_0_.2, bf16[64,8192]{1,0:T(8,128)(2,1)} %copy-done.2, bf16[64,8192]{1,0:T(8,128)(2,1)} %copy-done.8, bf16[64,8192]{1,0:T(8,128)(2,1)} %copy-done.6, ...), custom_call_target="tpu_custom_call", output_to_operand_aliasing={{}: (18, {})} | custom-call | flops 134217728 | bytes 2097152 | tf_op jit(solution)/shard_map/shrink/pallas_call | solution.py:99
  122.7 24.1 %all-to-all-done.refs_3_ = bf16[16,14,48,128]{3,2,1,0:T(8,128)(2,1)S(1)} async-done(((bf16[16,14,48,128]{3,2,1,0:T(8,128)(2,1)}), bf16[16,14,48,128]{3,2,1,0:T(8,128)(2,1)S(1)}, u32[]{:S(2)}, u32[]{:S(2)}) %all-to-all-start) | async-done | bytes 2752544 | tf_op jit(solution)/shard_map/all_to_all | solution.py:288
  146.8 4.9 %all-to-all-start.1 = ((bf16[16,18,16,128]{3,2,1,0:T(8,128)(2,1)}), bf16[16,18,16,128]{3,2,1,0:T(8,128)(2,1)}, u32[]{:S(2)}, u32[]{:S(2)}) async-start(bf16[16,18,16,128]{3,2,1,0:T(8,128)(2,1)} %shrink.1), calls=%async_computation.1 | async-start | bytes 2359296 | tf_op jit(solution)/shard_map/all_to_all | solution.py:305
  151.7 0.7 concatenate.8.scalars
  152.4 23.5 %base.3.refs_1_ = f32[512,1792]{1,0:T(8,128)} custom-call(bf16[64,8192]{1,0:T(8,128)(2,1)} %collective-permute-done.4.refs_8_.refs_0_, bf16[64,8192]{1,0:T(8,128)(2,1)} %copy-done.3, bf16[64,8192]{1,0:T(8,128)(2,1)} %collective-permute-done.10.refs_10_.refs_2_, bf16[64,8192]{1,0:T(8,128)(2,1)} %collective-permute-done.11.refs_11_.refs_3_, ...), custom_call_target="tpu_custom_call" | custom-call | flops 15032385536 | bytes 41418752 | tf_op jit(solution)/shard_map/base/pallas_call | solution.py:145
  175.9 3.7 %all-to-all-done.1.refs_2_.refs_4_ = bf16[16,18,16,128]{3,2,1,0:T(8,128)(2,1)} async-done(((bf16[16,18,16,128]{3,2,1,0:T(8,128)(2,1)}), bf16[16,18,16,128]{3,2,1,0:T(8,128)(2,1)}, u32[]{:S(2)}, u32[]{:S(2)}) %all-to-all-start.1) | async-done | bytes 1179680 | tf_op jit(solution)/shard_map/all_to_all | solution.py:305
  179.6 11.3 %last.1 = bf16[1024,1792]{1,0:T(8,128)(2,1)} custom-call(s32[32]{0:T(128)} %concatenate.8.scalars, f32[512,1792]{1,0:T(8,128)} %base.2.refs_0_, f32[512,1792]{1,0:T(8,128)} %base.3.refs_1_, bf16[16,18,16,128]{3,2,1,0:T(8,128)(2,1)} %all-to-all-done.1.refs_2_.refs_4_, bf16[16,14,48,128]{3,2,1,0:T(8,128)(2,1)} %copy-done, ...), custom_call_target="tpu_custom_call" | custom-call | flops 3758096384 | bytes 14680064 | tf_op jit(solution)/shard_map/last/pallas_call | solution.py:201
  (40 shorter events, 1.4 us)
Async XLA Ops:
  0.0 52.3 %copy-start.1 = (bf16[64,8192]{1,0:T(8,128)(2,1)S(1)}, bf16[64,8192]{1,0:T(8,128)(2,1)}, u32[]{:S(2)}) copy-start(bf16[64,8192]{1,0:T(8,128)(2,1)} %refs_0_.2) | copy-start | bytes 3145732
  0.0 24.2 %collective-permute-start.1 = (bf16[64,8192]{1,0:T(8,128)(2,1)}, bf16[64,8192]{1,0:T(8,128)(2,1)S(1)}, u32[]{:S(2)}, u32[]{:S(2)}) collective-permute-start(bf16[64,8192]{1,0:T(8,128)(2,1)} %refs_0_.2), channel_id=1, source_target_pairs={{0,2},{1,3},{2,0},{3,1},{4,6},{5,7},{6,4},{7,5},{8,10},{9,11},{10,... | collective-permute-start | bytes 3145736 | tf_op jit(solution)/shard_map/ppermute | solution.py:263
  0.2 24.1 %collective-permute-start = (bf16[64,8192]{1,0:T(8,128)(2,1)}, bf16[64,8192]{1,0:T(8,128)(2,1)S(1)}, u32[]{:S(2)}, u32[]{:S(2)}) collective-permute-start(bf16[64,8192]{1,0:T(8,128)(2,1)} %refs_0_.2), channel_id=1, source_target_pairs={{0,4},{1,5},{2,6},{3,7},{4,12},{5,13},{6,14},{7,15},{8,0},{9,1},{1... | collective-permute-start | bytes 3145736 | tf_op jit(solution)/shard_map/ppermute | solution.py:263
  24.2 54.1 %copy-start.2 = (bf16[64,8192]{1,0:T(8,128)(2,1)}, bf16[64,8192]{1,0:T(8,128)(2,1)S(1)}, u32[]{:S(2)}) copy-start(bf16[64,8192]{1,0:T(8,128)(2,1)S(1)} %collective-permute-done.1.refs_1_) | copy-start | bytes 3145732
  24.4 52.9 %copy-start.4 = (bf16[64,8192]{1,0:T(8,128)(2,1)}, bf16[64,8192]{1,0:T(8,128)(2,1)S(1)}, u32[]{:S(2)}) copy-start(bf16[64,8192]{1,0:T(8,128)(2,1)S(1)} %collective-permute-done.refs_4_) | copy-start | bytes 3145732
  24.4 22.9 %collective-permute-start.5 = (bf16[64,8192]{1,0:T(8,128)(2,1)S(1)}, bf16[64,8192]{1,0:T(8,128)(2,1)S(1)}, u32[]{:S(2)}, u32[]{:S(2)}) collective-permute-start(bf16[64,8192]{1,0:T(8,128)(2,1)S(1)} %collective-permute-done.refs_4_), channel_id=1, source_target_pairs={{0,2},{1,3},{2,0},{3,1},{4,6},{5,7},{6,4},{7,5},{8,10},{9,11},{10,... | collective-permute-start | bytes 3145736 | tf_op jit(solution)/shard_map/ppermute | solution.py:263
  25.6 23.3 %collective-permute-start.4 = (bf16[64,8192]{1,0:T(8,128)(2,1)S(1)}, bf16[64,8192]{1,0:T(8,128)(2,1)}, u32[]{:S(2)}, u32[]{:S(2)}) collective-permute-start(bf16[64,8192]{1,0:T(8,128)(2,1)S(1)} %collective-permute-done.refs_4_), channel_id=1, source_target_pairs={{0,4},{1,5},{2,6},{3,7},{4,12},{5,13},{6,14},{7,15},{8,0},{9,1},{1... | collective-permute-start | bytes 3145736 | tf_op jit(solution)/shard_map/ppermute | solution.py:263
  28.6 27.4 %collective-permute-start.3 = (bf16[64,8192]{1,0:T(8,128)(2,1)S(1)}, bf16[64,8192]{1,0:T(8,128)(2,1)S(1)}, u32[]{:S(2)}, u32[]{:S(2)}) collective-permute-start(bf16[64,8192]{1,0:T(8,128)(2,1)S(1)} %collective-permute-done.1.refs_1_), channel_id=1, source_target_pairs={{0,1},{1,0},{2,3},{3,2},{4,5},{5,4},{6,7},{7,6},{8,9},{9,8},{10,11... | collective-permute-start | bytes 3145736 | tf_op jit(solution)/shard_map/ppermute | solution.py:263
  31.0 25.0 %collective-permute-start.6 = (bf16[64,8192]{1,0:T(8,128)(2,1)S(1)}, bf16[64,8192]{1,0:T(8,128)(2,1)S(1)}, u32[]{:S(2)}, u32[]{:S(2)}) collective-permute-start(bf16[64,8192]{1,0:T(8,128)(2,1)S(1)} %collective-permute-done.refs_4_), channel_id=1, source_target_pairs={{0,1},{1,0},{2,3},{3,2},{4,5},{5,4},{6,7},{7,6},{8,9},{9,8},{10,11... | collective-permute-start | bytes 3145736 | tf_op jit(solution)/shard_map/ppermute | solution.py:263
  47.3 30.0 %copy-start.5 = (bf16[64,8192]{1,0:T(8,128)(2,1)}, bf16[64,8192]{1,0:T(8,128)(2,1)S(1)}, u32[]{:S(2)}) copy-start(bf16[64,8192]{1,0:T(8,128)(2,1)S(1)} %collective-permute-done.5.refs_5_) | copy-start | bytes 3145732
  48.9 21.9 %collective-permute-start.9 = (bf16[64,8192]{1,0:T(8,128)(2,1)}, bf16[64,8192]{1,0:T(8,128)(2,1)S(1)}, u32[]{:S(2)}, u32[]{:S(2)}) collective-permute-start(bf16[64,8192]{1,0:T(8,128)(2,1)} %collective-permute-done.4.refs_8_.refs_0_), channel_id=1, source_target_pairs={{0,2},{1,3},{2,0},{3,1},{4,6},{5,7},{6,4},{7,5},{8,10},{9,11},{10,... | collective-permute-start | bytes 3145736 | tf_op jit(solution)/shard_map/ppermute | solution.py:263
  49.1 22.6 %collective-permute-start.8 = (bf16[64,8192]{1,0:T(8,128)(2,1)}, bf16[64,8192]{1,0:T(8,128)(2,1)}, u32[]{:S(2)}, u32[]{:S(2)}) collective-permute-start(bf16[64,8192]{1,0:T(8,128)(2,1)} %collective-permute-done.4.refs_8_.refs_0_), channel_id=1, source_target_pairs={{0,4},{1,5},{2,6},{3,7},{4,12},{5,13},{6,14},{7,15},{8,0},{9,1},{1... | collective-permute-start | bytes 3145736 | tf_op jit(solution)/shard_map/ppermute | solution.py:263
  52.3 24.9 %collective-permute-start.2 = (bf16[64,8192]{1,0:T(8,128)(2,1)S(1)}, bf16[64,8192]{1,0:T(8,128)(2,1)S(1)}, u32[]{:S(2)}, u32[]{:S(2)}) collective-permute-start(bf16[64,8192]{1,0:T(8,128)(2,1)S(1)} %copy-done.1), channel_id=1, source_target_pairs={{0,1},{1,0},{2,3},{3,2},{4,5},{5,4},{6,7},{7,6},{8,9},{9,8},{10,11... | collective-permute-start | bytes 3145736 | tf_op jit(solution)/shard_map/ppermute | solution.py:263
  56.0 21.3 %copy-start.6 = (bf16[64,8192]{1,0:T(8,128)(2,1)}, bf16[64,8192]{1,0:T(8,128)(2,1)S(1)}, u32[]{:S(2)}) copy-start(bf16[64,8192]{1,0:T(8,128)(2,1)S(1)} %collective-permute-done.3.refs_3_) | copy-start | bytes 3145732
  56.0 22.3 %collective-permute-start.7 = (bf16[64,8192]{1,0:T(8,128)(2,1)S(1)}, bf16[64,8192]{1,0:T(8,128)(2,1)}, u32[]{:S(2)}, u32[]{:S(2)}) collective-permute-start(bf16[64,8192]{1,0:T(8,128)(2,1)S(1)} %collective-permute-done.5.refs_5_), channel_id=1, source_target_pairs={{0,1},{1,0},{2,3},{3,2},{4,5},{5,4},{6,7},{7,6},{8,9},{9,8},{10,11... | collective-permute-start | bytes 3145736 | tf_op jit(solution)/shard_map/ppermute | solution.py:263
  56.1 21.2 %copy-start.7 = (bf16[64,8192]{1,0:T(8,128)(2,1)}, bf16[64,8192]{1,0:T(8,128)(2,1)S(1)}, u32[]{:S(2)}) copy-start(bf16[64,8192]{1,0:T(8,128)(2,1)S(1)} %collective-permute-done.6.refs_6_) | copy-start | bytes 3145732
  56.1 62.2 %collective-permute-start.10 = (bf16[64,8192]{1,0:T(8,128)(2,1)}, bf16[64,8192]{1,0:T(8,128)(2,1)}, u32[]{:S(2)}, u32[]{:S(2)}) collective-permute-start(bf16[64,8192]{1,0:T(8,128)(2,1)} %collective-permute-done.4.refs_8_.refs_0_), channel_id=1, source_target_pairs={{0,1},{1,0},{2,3},{3,2},{4,5},{5,4},{6,7},{7,6},{8,9},{9,8},{10,11... | collective-permute-start | bytes 3145736 | tf_op jit(solution)/shard_map/ppermute | solution.py:263
  70.8 6.5 %copy-start.3 = (bf16[64,8192]{1,0:T(8,128)(2,1)}, bf16[64,8192]{1,0:T(8,128)(2,1)S(1)}, u32[]{:S(2)}) copy-start(bf16[64,8192]{1,0:T(8,128)(2,1)S(1)} %collective-permute-done.9.refs_9_.refs_1_) | copy-start | bytes 3145732
  71.8 46.5 %collective-permute-start.13 = (bf16[64,8192]{1,0:T(8,128)(2,1)}, bf16[64,8192]{1,0:T(8,128)(2,1)}, u32[]{:S(2)}, u32[]{:S(2)}) collective-permute-start(bf16[64,8192]{1,0:T(8,128)(2,1)} %collective-permute-done.8.refs_12_.refs_4_), channel_id=1, source_target_pairs={{0,1},{1,0},{2,3},{3,2},{4,5},{5,4},{6,7},{7,6},{8,9},{9,8},{10,11... | collective-permute-start | bytes 3145736 | tf_op jit(solution)/shard_map/ppermute | solution.py:263
  76.0 33.2 %collective-permute-start.12 = (bf16[64,8192]{1,0:T(8,128)(2,1)}, bf16[64,8192]{1,0:T(8,128)(2,1)}, u32[]{:S(2)}, u32[]{:S(2)}) collective-permute-start(bf16[64,8192]{1,0:T(8,128)(2,1)} %collective-permute-done.8.refs_12_.refs_4_), channel_id=1, source_target_pairs={{0,2},{1,3},{2,0},{3,1},{4,6},{5,7},{6,4},{7,5},{8,10},{9,11},{10,... | collective-permute-start | bytes 3145736 | tf_op jit(solution)/shard_map/ppermute | solution.py:263
  77.3 1.0 copy-start.8
  78.3 68.5 %all-to-all-start = ((bf16[16,14,48,128]{3,2,1,0:T(8,128)(2,1)}), bf16[16,14,48,128]{3,2,1,0:T(8,128)(2,1)S(1)}, u32[]{:S(2)}, u32[]{:S(2)}) async-start(bf16[16,14,48,128]{3,2,1,0:T(8,128)(2,1)} %get-tuple-element.49), calls=%async_computation | async-start | bytes 5505024 | tf_op jit(solution)/shard_map/all_to_all | solution.py:288
  85.3 28.3 %copy-start.10 = (s32[16]{0:T(128)S(1)}, s32[16]{0:T(128)}, u32[]{:S(2)}) copy-start(s32[16]{0:T(128)} %param.11) | copy-start | bytes 196
  85.3 28.4 %copy-start.9 = (s32[16]{0:T(128)S(1)}, s32[16]{0:T(128)}, u32[]{:S(2)}) copy-start(s32[16]{0:T(128)} %param.12) | copy-start | bytes 196
  85.3 32.9 %collective-permute-start.11 = (bf16[64,8192]{1,0:T(8,128)(2,1)}, bf16[64,8192]{1,0:T(8,128)(2,1)}, u32[]{:S(2)}, u32[]{:S(2)}) collective-permute-start(bf16[64,8192]{1,0:T(8,128)(2,1)} %copy-done.3), channel_id=1, source_target_pairs={{0,1},{1,0},{2,3},{3,2},{4,5},{5,4},{6,7},{7,6},{8,9},{9,8},{10,11... | collective-permute-start | bytes 3145736 | tf_op jit(solution)/shard_map/ppermute | solution.py:263
  109.2 9.0 %collective-permute-start.14 = (bf16[64,8192]{1,0:T(8,128)(2,1)}, bf16[64,8192]{1,0:T(8,128)(2,1)}, u32[]{:S(2)}, u32[]{:S(2)}) collective-permute-start(bf16[64,8192]{1,0:T(8,128)(2,1)} %collective-permute-done.12.refs_13_.refs_5_), channel_id=1, source_target_pairs={{0,1},{1,0},{2,3},{3,2},{4,5},{5,4},{6,7},{7,6},{8,9},{9,8},{10,11... | collective-permute-start | bytes 3145736 | tf_op jit(solution)/shard_map/ppermute | solution.py:263
  146.8 29.1 %copy-start = (bf16[16,14,48,128]{3,2,1,0:T(8,128)(2,1)}, bf16[16,14,48,128]{3,2,1,0:T(8,128)(2,1)S(1)}, u32[]{:S(2)}) copy-start(bf16[16,14,48,128]{3,2,1,0:T(8,128)(2,1)S(1)} %all-to-all-done.refs_3_) | copy-start | bytes 8257540
  146.8 32.8 %all-to-all-start.1 = ((bf16[16,18,16,128]{3,2,1,0:T(8,128)(2,1)}), bf16[16,18,16,128]{3,2,1,0:T(8,128)(2,1)}, u32[]{:S(2)}, u32[]{:S(2)}) async-start(bf16[16,18,16,128]{3,2,1,0:T(8,128)(2,1)} %shrink.1), calls=%async_computation.1 | async-start | bytes 2359296 | tf_op jit(solution)/shard_map/all_to_all | solution.py:305
